TPU v7x, 32 devices: a whole 2x2x4 slice. The times are simulated.
32 devices in a mesh: section: 2 (over core), dp: 4 (over z), ctx: 4 (over y, x).
Axes of the slice: x: 2, y: 2, z: 4, core: 2. Of those that a mesh axis runs over, the one named last changes fastest.
Arguments:
- hidden: bfloat16 [2, 4, 1024, 1024], P(None, 'dp', 'ctx'), may hold values from -6 to 6
- cotangent: bfloat16 [2, 4, 1024, 1024], P(None, 'dp', 'ctx'), may hold values from -6 to 6
- segments: int32 [2, 4, 1024], P(None, 'dp'), may hold values from 0 to 2, as said below
- in_weight: bfloat16 [2, 1024, 4384], P('section', ('dp', 'ctx')), may hold values from -0.1875 to 0.1875
- out_weight: bfloat16 [2, 2048, 1024], P('section', ('dp', 'ctx')), may hold values from -0.125 to 0.125
- conv_weight: bfloat16 [2, 4, 2304], P('section', None, ('dp', 'ctx')), may hold values from -3 to 3
- conv_bias: bfloat16 [2, 2304], P('section', ('dp', 'ctx')), may hold values from -3 to 3
- norm_gain: bfloat16 [2, 1024], P('section', ('dp', 'ctx')), may hold values from 0.25 to 1.75
- gate_gain: bfloat16 [2, 2048], P('section', ('dp', 'ctx')), may hold values from 0.25 to 1.75
- step_bias: float32 [2, 32], P('section'), may hold values from -7 to -3
- decay_log: float32 [2, 32], P('section'), may hold values from -1.5 to 0.5
- skip_gain: float32 [2, 32], P('section'), may hold values from 0.5 to 1.5
Outputs:
- layer_out: bfloat16 [2, 2, 4, 1024, 1024], P('section', None, 'dp', 'ctx')
- input_grad: bfloat16 [2, 2, 4, 1024, 1024], P('section', None, 'dp', 'ctx')
- in_weight_grad: float32 [2, 1024, 4384], P('section', ('dp', 'ctx'))
- out_weight_grad: float32 [2, 2048, 1024], P('section', ('dp', 'ctx'))
- conv_weight_grad: float32 [2, 4, 2304], P('section', None, ('dp', 'ctx'))
- conv_bias_grad: float32 [2, 2304], P('section', ('dp', 'ctx'))
- norm_gain_grad: float32 [2, 1024], P('section', ('dp', 'ctx'))
- gate_gain_grad: float32 [2, 2048], P('section', ('dp', 'ctx'))
- step_bias_grad: float32 [2, 32], P('section')
- decay_log_grad: float32 [2, 32], P('section')
- skip_gain_grad: float32 [2, 32], P('section')
Inputs may be any that keep to these rules, and one draw needn't show every extreme that they name: `segments`: in every row the numbers start at 0, never fall, and rise by one at exactly two tokens: one among the first 256 tokens of the row but not its first token, and one among its last 256 tokens but not the first of those.
All inputs are finite; a program needn't handle non-finite values.
Results may differ from a plain program's by a relative error of at most 0.012.
Values may be sent and summed in bfloat16 or wider, within the bound.
No kernel may reach another device: no remote copies, remote signals or barrier semaphores. Data moves between devices by JAX's collectives and lax.ppermute only.
A program may use at most 320 MiB of HBM per device.

v0:
```python
from functools import reduce

import jax
import jax.numpy as jnp
from jax import lax
from jax.sharding import PartitionSpec as P

D = 1024
E = 2048
H = 32
P_SIZE = 64
N = 128
KW = 4
CC = 2304
NPROJ = 4384


eps_norm = 1e-05
precise = lax.Precision.HIGHEST


def shifted(shard, axis, by):
    length = lax.axis_size(axis)
    pairs = [(i, i + by) for i in range(length) if 0 <= i + by < length]
    return lax.ppermute(shard, axis, pairs)


def prefix(shard, axis, combine, identity):
    length, position = (lax.axis_size(axis), lax.axis_index(axis))
    everything = jax.tree.map(
        lambda part, kind: lax.all_gather(part.astype(kind), axis),
        shard,
        (jnp.bfloat16, jnp.bfloat16),
    )
    start = jax.tree.map(
        lambda part, zero: jnp.broadcast_to(jnp.asarray(zero, part.dtype), part.shape),
        shard,
        identity,
    )

    def step(k, before):
        reached = k < position
        new = combine(
            before, jax.tree.map(lambda part, own: part[k].astype(own.dtype), everything, shard)
        )
        return jax.tree.map(lambda a, b: jnp.where(reached, a, b), new, before)

    return lax.fori_loop(0, length, step, start)


def prefix_2(shard, axis, join, neutral):
    count = lax.axis_size(axis)
    place = lax.axis_index(axis)
    ahead = count - 1 - place
    gathered = jax.tree.map(
        lambda a, kind: lax.all_gather(a.astype(kind), axis),
        shard,
        jax.tree.map(lambda a: jnp.bfloat16 if a.dtype == jnp.float32 else a.dtype, shard),
    )
    state = jax.tree.map(lambda a, e: jnp.zeros_like(a) + jnp.asarray(e, a.dtype), shard, neutral)

    def one(step, state):
        source = count - 1 - step
        return join(
            state,
            jax.tree.map(
                lambda a, own: lax.dynamic_index_in_dim(a, source, 0, False).astype(own.dtype),
                gathered,
                shard,
            ),
        )

    return lax.fori_loop(0, ahead, one, state)


def rms_scale(values):
    return values * lax.rsqrt(jnp.mean(values * values, axis=-1, keepdims=True) + eps_norm)


def norm_input(values, gain_vec):
    return rms_scale(values) * gain_vec


def chain_link(earlier, later):
    return (earlier[0] * later[0], later[0][..., None, None] * earlier[1] + later[1])


def add_trees(left, right):
    return jax.tree.map(jnp.add, left, right)


def times_transposed(left, right):
    return lax.dot_general(
        left, right, (((1,), (1,)), ((), ())), preferred_element_type=jnp.float32
    )


def conv_state(extended, raw_step, seg_ext, tap_values, tap_bias, step_bias, decay_log):
    length = raw_step.shape[0]
    seg_now = seg_ext[KW - 1 :]
    summed = jnp.broadcast_to(tap_bias, (length, tap_bias.shape[0]))
    for offset in range(KW):
        same_seg = (seg_ext[offset : offset + length] == seg_now).astype(jnp.float32)
        summed = (
            summed + tap_values[offset] * extended[offset : offset + length] * same_seg[:, None]
        )
    active = jax.nn.silu(summed)
    inputs = active[:, :E].reshape(length, H, P_SIZE)
    writer = active[:, E : E + N]
    reader = active[:, E + N :]
    step_size = jax.nn.softplus(raw_step + step_bias)
    cumulative = jnp.cumsum(-step_size * jnp.exp(decay_log), axis=0)
    keep_end = (seg_now == seg_now[-1]).astype(jnp.float32)
    end_weight = jnp.exp(cumulative[-1][None, :] - cumulative) * keep_end[:, None]
    scaled = inputs * step_size[:, :, None]
    end_state = jnp.einsum(
        "shp,sn->hpn", scaled * end_weight[:, :, None], writer, precision=precise
    )
    fading = jnp.exp(cumulative[-1]) * (seg_now[-1] == seg_ext[KW - 2]).astype(jnp.float32)
    return (fading, end_state, (inputs, writer, reader, step_size, cumulative))


def state_output(extras, memory, gate_pre, seg_ext, gate_vec, skip_vec):
    inputs, writer, reader, step_size, cumulative = extras
    length = step_size.shape[0]
    seg_now = seg_ext[KW - 1 :]
    row_ids = jnp.arange(length)
    causal_mask = (row_ids[:, None] >= row_ids[None, :]) & (seg_now[:, None] == seg_now[None, :])
    cum_heads = cumulative.T
    log_gaps = cum_heads[:, :, None] - cum_heads[:, None, :]
    fading = jnp.exp(jnp.where(causal_mask[None, :, :], log_gaps, -1e30))
    scores = jnp.dot(reader, writer.T, precision=precise)
    scaled = jnp.transpose(inputs * step_size[:, :, None], (1, 0, 2))
    mixed_heads = jnp.einsum("hts,hsp->htp", scores[None, :, :] * fading, scaled, precision=precise)
    mixed_out = jnp.transpose(mixed_heads, (1, 0, 2))
    carry_in = jnp.exp(cumulative) * (seg_now == seg_ext[KW - 2]).astype(jnp.float32)[:, None]
    mixed_out = mixed_out + carry_in[:, :, None] * jnp.einsum(
        "tn,hpn->thp", reader, memory, precision=precise
    )
    mixed_out = mixed_out + skip_vec[None, :, None] * inputs
    gated_out = mixed_out.reshape(length, E) * jax.nn.silu(gate_pre)
    return rms_scale(gated_out) * gate_vec


def at_tick(stacked, tick_index):
    return lax.dynamic_index_in_dim(stacked, tick_index, 0, keepdims=False)


def shards(
    hidden,
    cotangent,
    segments,
    in_weight,
    out_weight,
    conv_weight,
    conv_bias,
    norm_gain,
    gate_gain,
    step_bias,
    decay_log,
    skip_gain,
):
    section_id = lax.axis_index("section")
    ctx_id = lax.axis_index("ctx")
    batches, rows_here, tokens = (hidden.shape[0], hidden.shape[1], hidden.shape[2])
    conv_local = jnp.swapaxes(conv_weight, 1, 2)
    fetched = (
        lax.all_gather(in_weight, ("dp", "ctx"), axis=1, tiled=True),
        lax.all_gather(out_weight, ("dp", "ctx"), axis=1, tiled=True),
        lax.all_gather(conv_local, ("dp", "ctx"), axis=1, tiled=True),
        lax.all_gather(conv_bias, ("dp", "ctx"), axis=1, tiled=True),
        lax.all_gather(norm_gain, ("dp", "ctx"), axis=1, tiled=True),
        lax.all_gather(gate_gain, ("dp", "ctx"), axis=1, tiled=True),
    )
    in_full = fetched[0][0]
    out_full = fetched[1][0]
    conv_taps = fetched[2][0].T.astype(jnp.float32)
    conv_shift = fetched[3][0].astype(jnp.float32)
    norm_vec = fetched[4][0].astype(jnp.float32)
    gate_vec = fetched[5][0].astype(jnp.float32)
    step_vec = step_bias[0]
    decay_vec = decay_log[0]
    skip_vec = skip_gain[0]
    lead_pad = jnp.full((batches, rows_here, KW - 1), -1, jnp.int32)
    seg_all = lax.dynamic_slice_in_dim(
        jnp.concatenate([lead_pad, segments], axis=2), ctx_id * tokens, tokens + KW - 1, 2
    )
    conv_part = jax.vmap(conv_state, in_axes=(0, 0, 0, None, None, None, None))
    out_part = jax.vmap(state_output, in_axes=(0, 0, 0, 0, None, None))
    source = hidden.astype(jnp.float32)
    is_first = section_id == 0
    arriving = jnp.zeros_like(source[0])
    sent_list = []
    kept_ticks = []
    for timestep in range(batches + 1):
        own_batch = jnp.clip(timestep - section_id, 0, batches - 1)
        residual = jnp.where(is_first, source[min(timestep, batches - 1)], arriving)
        run_seg_ext = at_tick(seg_all, own_batch)
        normed = norm_input(residual, norm_vec).astype(jnp.bfloat16)
        run_projected = jnp.dot(
            normed.reshape(-1, D), in_full, preferred_element_type=jnp.float32
        ).reshape(rows_here, tokens, NPROJ)
        conv_in = run_projected[:, :, E : E + CC].astype(jnp.bfloat16)
        edge_rows = shifted(conv_in[:, tokens - KW + 1 :], "ctx", 1)
        run_extended = jnp.concatenate([edge_rows, conv_in], axis=1).astype(jnp.float32)
        run_fading, run_end_state, run_extras = conv_part(
            run_extended,
            run_projected[:, :, E + CC :],
            run_seg_ext,
            conv_taps,
            conv_shift,
            step_vec,
            decay_vec,
        )
        run_chained = prefix(
            (run_fading, run_end_state),
            "ctx",
            chain_link,
            (jnp.ones_like(run_fading), jnp.zeros_like(run_end_state)),
        )
        run_memory = run_chained[1]
        normed_out = out_part(
            run_extras, run_memory, run_projected[:, :, :E], run_seg_ext, gate_vec, skip_vec
        ).astype(jnp.bfloat16)
        branch = jnp.dot(
            normed_out.reshape(-1, E), out_full, preferred_element_type=jnp.float32
        ).reshape(rows_here, tokens, D)
        result = residual + branch
        saved_vals = (residual, normed, run_projected, run_extended, run_memory, normed_out)
        leaving = result.astype(jnp.bfloat16)
        sent_list.append(leaving)
        kept_ticks.append(saved_vals)
        if timestep < batches:
            arriving = shifted(leaving, "section", 1).astype(jnp.float32)
    resid_s, normed_s, proj_s, ext_s, memory_s, outn_s = [
        jnp.stack(column) for column in zip(*kept_ticks)
    ]
    refetched = (
        lax.all_gather(in_weight, ("dp", "ctx"), axis=1, tiled=True),
        lax.all_gather(out_weight, ("dp", "ctx"), axis=1, tiled=True),
    )
    back_in = refetched[0][0]
    back_out = refetched[1][0]

    def run_backward(grad_out, residual, seg_ext, projected, extended, memory):
        grad_low = grad_out.astype(jnp.bfloat16)
        d_normed_out = times_transposed(grad_low.reshape(-1, D), back_out).reshape(
            rows_here, tokens, E
        )

        def conv_fn(ext_rows, raw_rows, tap_values, tap_bias, step_vals, decay_vals):
            return conv_part(
                ext_rows, raw_rows, seg_ext, tap_values, tap_bias, step_vals, decay_vals
            )

        def out_fn(extra_vals, mem_vals, gate_rows, gate_vals, skip_vals):
            return out_part(extra_vals, mem_vals, gate_rows, seg_ext, gate_vals, skip_vals)

        (fading, end_state, extras), pull_conv = jax.vjp(
            conv_fn, extended, projected[:, :, E + CC :], conv_taps, conv_shift, step_vec, decay_vec
        )
        _, pull_out = jax.vjp(out_fn, extras, memory, projected[:, :, :E], gate_vec, skip_vec)
        d_extras, d_memory, d_gate, d_gate_vec, d_skip = pull_out(d_normed_out)
        chained = prefix_2(
            (fading, d_memory), "ctx", chain_link, (jnp.ones_like(fading), jnp.zeros_like(d_memory))
        )
        later_grad = chained[1]
        d_fading = jnp.sum(later_grad * memory, axis=(2, 3))
        d_ext, d_raw, d_taps, d_shift, d_step, d_decay = pull_conv((d_fading, later_grad, d_extras))
        edge_back = shifted(d_ext[:, : KW - 1], "ctx", -1)
        d_conv = d_ext[:, KW - 1 :] + jnp.pad(edge_back, ((0, 0), (tokens - KW + 1, 0), (0, 0)))
        d_proj = jnp.concatenate([d_gate, d_conv, d_raw], axis=2).astype(jnp.bfloat16)
        d_normed = times_transposed(d_proj.reshape(-1, NPROJ), back_in).reshape(
            rows_here, tokens, D
        )
        _, pull_norm = jax.vjp(norm_input, residual, norm_vec)
        d_resid, d_norm_vec = pull_norm(d_normed)
        return (
            grad_out + d_resid,
            grad_low,
            d_proj,
            (d_taps, d_shift, d_norm_vec, d_gate_vec, d_step, d_decay, d_skip),
        )

    incoming = cotangent.astype(jnp.float32)
    returning = jnp.zeros_like(incoming[0])
    grads_back = []
    low_grads = []
    proj_grads = []
    small_grads = []
    for timestep in range(batches + 1):
        position = timestep - 1 + section_id
        own_batch = jnp.clip(position, 0, batches - 1)
        is_valid = ((position >= 0) & (position < batches)).astype(jnp.float32)
        grad_out = is_valid * jnp.where(is_first, returning, incoming[min(timestep, batches - 1)])
        fwd_step = own_batch + section_id
        d_resid, grad_low, d_proj, small_vals = run_backward(
            grad_out,
            at_tick(resid_s, fwd_step),
            at_tick(seg_all, own_batch),
            at_tick(proj_s, fwd_step),
            at_tick(ext_s, fwd_step),
            at_tick(memory_s, fwd_step),
        )
        leaving = d_resid.astype(jnp.bfloat16)
        grads_back.append(leaving)
        low_grads.append(grad_low)
        proj_grads.append(d_proj)
        small_grads.append(small_vals)
        if timestep < batches:
            returning = shifted(leaving, "section", -1).astype(jnp.float32)
    totals = reduce(add_trees, small_grads)
    normed_all = lax.dynamic_slice_in_dim(normed_s, section_id, batches, 0)
    outn_all = lax.dynamic_slice_in_dim(outn_s, section_id, batches, 0)
    dproj_all = lax.dynamic_slice_in_dim(jnp.stack(proj_grads), 1 - section_id, batches, 0)
    glow_all = lax.dynamic_slice_in_dim(jnp.stack(low_grads), 1 - section_id, batches, 0)
    d_in_w = lax.dot_general(
        normed_all.reshape(-1, D),
        dproj_all.reshape(-1, NPROJ),
        (((0,), (0,)), ((), ())),
        preferred_element_type=jnp.float32,
    )
    d_out_w = lax.dot_general(
        outn_all.reshape(-1, E),
        glow_all.reshape(-1, D),
        (((0,), (0,)), ((), ())),
        preferred_element_type=jnp.float32,
    )
    taps_grad = totals[0].T
    shares = (
        lax.psum_scatter(d_in_w[None], ("dp", "ctx"), scatter_dimension=1, tiled=True),
        lax.psum_scatter(d_out_w[None], ("dp", "ctx"), scatter_dimension=1, tiled=True),
        lax.psum_scatter(taps_grad[None], ("dp", "ctx"), scatter_dimension=1, tiled=True),
        lax.psum_scatter(totals[1][None], ("dp", "ctx"), scatter_dimension=1, tiled=True),
        lax.psum_scatter(totals[2][None], ("dp", "ctx"), scatter_dimension=1, tiled=True),
        lax.psum_scatter(totals[3][None], ("dp", "ctx"), scatter_dimension=1, tiled=True),
    )
    head_sums = lax.psum((totals[4][None], totals[5][None], totals[6][None]), ("dp", "ctx"))
    layer_out = lax.dynamic_slice_in_dim(jnp.stack(sent_list), section_id, batches, 0)[None]
    input_grad = lax.dynamic_slice_in_dim(jnp.stack(grads_back), 1 - section_id, batches, 0)[None]
    taps_share = jnp.swapaxes(shares[2], 1, 2)
    return (
        layer_out,
        input_grad,
        shares[0],
        shares[1],
        taps_share,
        shares[3],
        shares[4],
        shares[5],
        head_sums[0],
        head_sums[1],
        head_sums[2],
    )


def solution(mesh):
    in_specs = (
        P(None, "dp", "ctx", None),
        P(None, "dp", "ctx", None),
        P(None, "dp", None),
        P("section", ("dp", "ctx"), None),
        P("section", ("dp", "ctx"), None),
        P("section", None, ("dp", "ctx")),
        P("section", ("dp", "ctx")),
        P("section", ("dp", "ctx")),
        P("section", ("dp", "ctx")),
        P("section", None),
        P("section", None),
        P("section", None),
    )
    out_specs = (
        P("section", None, "dp", "ctx", None),
        P("section", None, "dp", "ctx", None),
        P("section", ("dp", "ctx"), None),
        P("section", ("dp", "ctx"), None),
        P("section", None, ("dp", "ctx")),
        P("section", ("dp", "ctx")),
        P("section", ("dp", "ctx")),
        P("section", ("dp", "ctx")),
        P("section", None),
        P("section", None),
        P("section", None),
    )
    return jax.shard_map(shards, mesh=mesh, in_specs=in_specs, out_specs=out_specs, check_vma=False)
```

profile of v0, /device:TPU:10, one launch (start us, length us, event | category | flops | bytes accessed | tf_op | source)
XLA Modules:
  0.0 2076.5 jit_solution(10109841514884972093)
XLA Ops:
  12.0 32.0 %all-reduce.47 = (bf16[1024]{0:T(1024)(128)(2,1)S(1)}, bf16[2304]{0:T(1024)(128)(2,1)S(1)}) all-reduce(bf16[1024]{0:T(1024)(128)(2,1)S(1)} %dynamic-update-slice.1, bf16[2304]{0:T(1024)(128)(2,1)S(1)} %dynamic-update-slice), channel_id=1, replica_groups=mesh['section'=2,'dp'=4,'ctx'=4] {'dp','ctx'}, use_global_device_ids=true, to_apply=%add.44 | all-reduce | flops 3328 | bytes 13312
  46.9 58.4 %all_gather.81 = bf16[1,2304,4]{2,0,1:T(2,128)(2,1)S(1)} all-gather(bf16[1,144,4]{2,0,1:T(2,128)(2,1)S(1)} %bitcast.1506), channel_id=1, replica_groups=mesh['section'=2,'dp'=4,'ctx'=4] {'dp','ctx'}, dimensions={1}, use_global_device_ids=true | all-gather | bytes 19584 | tf_op jit(solution)/shard_map/all_gather | solution.py:170
  110.6 34.8 %all-gather.15.cloned.1.call-done = bf16[1,1024,4384]{2,1,0:T(8,128)(2,1)} async-done(((bf16[1,64,4384]{2,1,0:T(8,128)(2,1)}), bf16[1,1024,4384]{2,1,0:T(8,128)(2,1)}) %all-gather.15.cloned.1.call-update) | async-done | bytes 8978448 | tf_op jit(solution)/shard_map/all_gather | solution.py:168
  145.4 8.8 bitcast_convert_fusion.8
  161.8 5.2 collective-permute-start
  180.6 29.3 %all_gather.87 = bf16[1,2048]{1,0:T(2,128)(2,1)S(1)} all-gather(bf16[1,128]{1,0:T(2,128)(2,1)S(1)} %copy-done.302), channel_id=1, replica_groups=mesh['section'=2,'dp'=4,'ctx'=4] {'dp','ctx'}, dimensions={1}, use_global_device_ids=true | all-gather | bytes 4352 | tf_op jit(solution)/shard_map/all_gather | solution.py:173
  210.6 9.3 all_gather.84
  224.8 7.9 while.87
  235.9 9.8 fusion.188
  249.4 45.2 %all-gather.17.cloned.1.call-done = bf16[1,2048,1024]{2,1,0:T(8,128)(2,1)} async-done(((bf16[1,128,1024]{2,1,0:T(8,128)(2,1)}), bf16[1,2048,1024]{2,1,0:T(8,128)(2,1)}) %all-gather.17.cloned.1.call-update) | async-done | bytes 4194320 | tf_op jit(solution)/shard_map/all_gather | solution.py:169
  294.5 12.5 fusion.268
  312.5 9.0 bitcast_convert_fusion.7
  356.2 7.3 all_gather.89
  367.7 13.7 all-gather.21.cloned.1.call-done
  381.3 5.5 while.88
  390.1 9.8 fusion.186
  420.0 9.5 bitcast_convert_fusion.6
  429.5 10.6 pad_maximum_fusion
  440.1 10.1 dynamic-slice_bitcast_fusion
  477.9 7.3 maximum_convert_fusion
  485.2 6.7 dynamic-slice_bitcast_fusion.3
  493.8 6.8 fusion.150
  506.5 7.6 all_gather.92
  514.1 8.5 all_gather.95
  522.6 8.2 all_gather.98
  559.1 11.6 fusion.151
  582.2 15.0 while.89
  603.1 9.7 fusion.183
  627.2 14.4 fusion.46
  658.4 9.9 fusion.182
  681.6 8.2 fusion.26
  690.9 6.3 while.84
  699.6 6.3 fusion.209
  708.1 5.3 multiply_reduce_fusion.14
  742.5 6.0 collective-permute-start.5
  757.2 7.3 fusion.331
  766.5 11.3 fusion.184
  781.1 4.9 multiply_reduce_fusion.16
  791.8 5.0 multiply_reduce_fusion.27
  796.8 11.2 fusion.181
  810.7 14.1 fusion.48
  835.6 8.6 fusion.21
  845.3 6.2 while.85
  854.1 6.3 fusion.201
  862.5 5.1 multiply_reduce_fusion.10
  894.9 7.0 collective-permute-start.7
  909.6 7.3 fusion.321
  925.5 5.1 fusion.528
  934.7 8.7 all_gather.101
  951.5 12.6 fusion.50
  973.4 8.2 fusion.16
  988.2 5.2 fusion.193
  995.4 4.9 multiply_reduce_fusion.6
  1027.4 4.8 collective-permute-start.9
  1047.2 7.6 fusion.311
  1058.5 23.2 %convolution_bitcast_fusion = f32[1,1024,4384]{1,2,0:T(8,128)} fusion(s32[]{:T(128)S(6)} %select_n.287, bf16[1,1,256,2048]{2,3,1,0:T(8,128)(2,1)} %bitcast.1484, bf16[1,1,256,2304]{2,3,1,0:T(8,128)(2,1)S(1)} %copy-done.98, bf16[1,1,256,32]{2,3,1,0:T(8,128)(2,1)S(1)} %copy-done.236, bf16[1,1,256,2048]{2,3,1,0:T(8,128)(2,1)} %bitcast.1486, ...), kind=kOutput, calls=%fused_computation.16 | convolution fusion | flops 4638408704 | bytes 26263560 | tf_op jit(solution)/shard_map/dot_general | solution.py:317
  1081.7 37.6 %copy.798 = f32[1,1024,4384]{2,0,1:T(1,128)} copy(f32[1,1024,4384]{1,2,0:T(8,128)} %convolution_bitcast_fusion) | data formatting | bytes 35913728 | tf_op jit(solution)/shard_map/broadcast_in_dim | solution.py:331
  1121.2 7.4 convolution_bitcast_fusion.1
  1139.4 30.0 %all-reduce.46 = (f32[1,32]{1,0:T(1,128)}, f32[1,32]{1,0:T(1,128)}, f32[1,32]{1,0:T(1,128)}) all-reduce(f32[1,32]{1,0:T(1,128)S(1)} %add_bitcast_fusion.2, f32[1,32]{1,0:T(1,128)S(1)} %bitcast_multiply_fusion.60, f32[1,32]{1,0:T(1,128)S(1)} %add_bitcast_fusion.1), channel_id=1, replica_groups=mesh['section'=2,'dp'=4,'ctx'=4] {'dp','ctx'}, use_global_device_ids=true, to_apply=%region_105.107 | all-reduce | flops 96 | bytes 768 | tf_op jit(solution)/shard_map/psum | solution.py:338
  1169.4 16.5 reduce-scatter.18.cloned.1.call-done
  1191.0 62.1 %reduce-scatter.20.cloned.1.call-done = f32[64,1]{1,0:T(8,128)} async-done(((f32[1024,1]{1,0:T(8,128)}), f32[64,1]{1,0:T(8,128)}) %reduce-scatter.20.cloned.1.call-update) | async-done | bytes 272
  1254.5 134.7 %reduce-scatter.16.cloned.1.call-done = f32[144,4]{1,0:T(8,128)} async-done(((f32[2304,4]{1,0:T(8,128)}), f32[144,4]{1,0:T(8,128)}) %reduce-scatter.16.cloned.1.call-update) | async-done | bytes 2320
  1390.7 494.7 %all-reduce.50.cloned.1.call-done = f32[1,1024,4384]{2,0,1:T(1,128)} async-done(((f32[1,1024,4384]{2,0,1:T(1,128)}), f32[1,1024,4384]{2,0,1:T(1,128)}) %all-reduce.50.cloned.1.call-update) | async-done | bytes 17956880
  1887.8 181.7 %reduce-scatter.14.cloned.1.call-done = f32[1,128,1024]{2,1,0:T(8,128)} async-done(((f32[1,2048,1024]{2,1,0:T(8,128)}), f32[1,128,1024]{2,1,0:T(8,128)}) %reduce-scatter.14.cloned.1.call-update) | async-done | bytes 524304 | tf_op jit(solution)/shard_map/reduce_scatter | solution.py:332
  (1071 shorter events, 487.0 us)
Async XLA Ops:
  7.2 36.9 %copy-start.258 = (s32[2,1,1024]{2,1,0:T(1,128)S(1)}, s32[2,1,1024]{2,1,0:T(1,128)}, u32[]{:S(2)}) copy-start(s32[2,1,1024]{2,1,0:T(1,128)} %param.27) | copy-start | bytes 24580
  7.2 39.5 %copy-start.296 = (bf16[1,4,144]{2,1,0:T(4,128)(2,1)S(1)}, bf16[1,4,144]{2,1,0:T(4,128)(2,1)}, u32[]{:S(2)}) copy-start(bf16[1,4,144]{2,1,0:T(4,128)(2,1)} %param.30) | copy-start | bytes 3460
  7.2 138.2 %all-gather.15.cloned.1.call-start = ((), (), s32[]{:S(2)}) async-start(), calls=%async_computation.5 | async-start | bytes 9748480 | tf_op jit(solution)/shard_map/all_gather | solution.py:168
  8.0 216.8 %all-gather.19.cloned.1.call-start = ((), (), s32[]{:S(2)}) async-start(), calls=%async_computation.8 | async-start | bytes 2621440 | tf_op jit(solution)/shard_map/all_gather | solution.py:31
  9.5 392.9 %copy-start.25 = (f32[2,1,256,1024]{3,2,1,0:T(8,128)}, f32[2,1,256,1024]{3,2,1,0:T(8,128)S(1)}, u32[]{:S(2)}) copy-start(f32[2,1,256,1024]{3,2,1,0:T(8,128)S(1)} %convert_element_type.558) | copy-start | bytes 6291460
  44.8 61.8 %copy-start.186 = (s32[1,259]{1,0:T(1,128)}, s32[1,259]{1,0:T(1,128)S(1)}, u32[]{:S(2)}) copy-start(s32[1,259]{1,0:T(1,128)S(1)} %get-tuple-element.1200) | copy-start | bytes 3112
  46.7 290.5 %copy-start.134 = (f32[2304]{0:T(1024)}, f32[2304]{0:T(1024)S(1)}, u32[]{:S(2)}) copy-start(f32[2304]{0:T(1024)S(1)} %convert_element_type.627) | copy-start | bytes 27652
  108.8 228.4 %copy-start.107 = (f32[2304]{0:T(1024)}, f32[2304]{0:T(1024)S(1)}, u32[]{:S(2)}) copy-start(f32[2304]{0:T(1024)S(1)} %get-tuple-element.994) | copy-start | bytes 27652
  108.8 228.4 %copy-start.112 = (f32[2304]{0:T(1024)}, f32[2304]{0:T(1024)S(1)}, u32[]{:S(2)}) copy-start(f32[2304]{0:T(1024)S(1)} %get-tuple-element.995) | copy-start | bytes 27652
  108.8 228.4 %copy-start.117 = (f32[2304]{0:T(1024)}, f32[2304]{0:T(1024)S(1)}, u32[]{:S(2)}) copy-start(f32[2304]{0:T(1024)S(1)} %get-tuple-element.996) | copy-start | bytes 27652
  108.9 45.4 %copy-start.218 = (f32[32]{0:T(128)}, f32[32]{0:T(128)S(1)}, u32[]{:S(2)}) copy-start(f32[32]{0:T(128)S(1)} %exponential_bitcast_fusion) | copy-start | bytes 388
  110.6 43.6 %copy-start.89 = (bf16[1,1,256,1024]{3,2,1,0:T(8,128)(2,1)}, bf16[1,1,256,1024]{3,2,1,0:T(8,128)(2,1)S(1)}, u32[]{:S(2)}) copy-start(bf16[1,1,256,1024]{3,2,1,0:T(8,128)(2,1)S(1)} %multiply_convert_fusion.5) | copy-start | bytes 1572868
  110.6 45.7 %copy-start.215 = (f32[1,32]{1,0:T(1,128)S(1)}, f32[1,32]{1,0:T(1,128)}, u32[]{:S(2)}) copy-start(f32[1,32]{1,0:T(1,128)} %param.34) | copy-start | bytes 388
  161.8 6.6 collective-permute-start
  176.9 33.7 %copy-start.300 = (bf16[1,1,32]{2,1,0:T(2,128)(2,1)S(1)}, bf16[1,1,32]{2,1,0:T(2,128)(2,1)}, u32[]{:S(2)}) copy-start(bf16[1,1,32]{2,1,0:T(2,128)(2,1)} %get-tuple-element.1186) | copy-start | bytes 196
  179.7 114.8 %all-gather.17.cloned.1.call-start = ((), (), s32[]{:S(2)}) async-start(), calls=%async_computation.6 | async-start | bytes 4456448 | tf_op jit(solution)/shard_map/all_gather | solution.py:169
  180.4 200.9 %all-gather.21.cloned.1.call-start = ((), (), s32[]{:S(2)}) async-start(), calls=%async_computation.9 | async-start | bytes 2621440 | tf_op jit(solution)/shard_map/all_gather | solution.py:31
  209.9 192.5 %copy-start.153 = (f32[1,2048]{1,0:T(1,128)}, f32[1,2048]{1,0:T(1,128)S(1)}, u32[]{:S(2)}) copy-start(f32[1,2048]{1,0:T(1,128)S(1)} %convert_element_type.625) | copy-start | bytes 24580
  249.4 57.7 %copy-start.276 = (f32[256]{0:T(256)}, f32[256]{0:T(256)S(1)}, u32[]{:S(2)}) copy-start(f32[256]{0:T(256)S(1)} %add_rsqrt_fusion.4) | copy-start | bytes 3076
  294.5 15.2 copy-start.187
  307.1 4.0 collective-permute-start.1
  329.0 5.7 collective-permute-start.2
  343.2 13.0 copy-start.299
  343.2 20.9 %copy-start.249 = (f32[32,2]{0,1:T(2,128)S(1)}, f32[32,2]{0,1:T(2,128)}, u32[]{:S(2)}) copy-start(f32[32,2]{0,1:T(2,128)} %copy-done.248) | copy-start | bytes 772
  345.9 236.3 %all-gather.23.cloned.1.call-start = ((), (), s32[]{:S(2)}) async-start(), calls=%async_computation.10 | async-start | bytes 2621440 | tf_op jit(solution)/shard_map/all_gather | solution.py:31
  405.4 11.7 collective-permute-start.3
  409.0 60.1 %copy-start.244 = (f32[1,256]{1,0:T(1,128)}, f32[1,256]{1,0:T(1,128)S(1)}, u32[]{:S(2)}) copy-start(f32[1,256]{1,0:T(1,128)S(1)} %get-tuple-element.1224) | copy-start | bytes 3076
  409.0 61.4 %copy-start.235 = (f32[1,256]{1,0:T(1,128)}, f32[1,256]{1,0:T(1,128)S(1)}, u32[]{:S(2)}) copy-start(f32[1,256]{1,0:T(1,128)S(1)} %get-tuple-element.1223) | copy-start | bytes 3076
  459.2 17.6 collective-permute-start.4
  505.2 184.6 %all-gather.25.cloned.1.call-start = ((), (), s32[]{:S(2)}) async-start(), calls=%async_computation.11 | async-start | bytes 2621440 | tf_op jit(solution)/shard_map/all_gather | solution.py:56
  627.2 217.1 %all-gather.27.cloned.1.call-start = ((), (), s32[]{:S(2)}) async-start(), calls=%async_computation.12 | async-start | bytes 2621440 | tf_op jit(solution)/shard_map/all_gather | solution.py:56
  627.2 14.4 copy-start.11
  627.2 14.4 copy-start.64
  742.5 8.2 collective-permute-start.5
  764.9 12.9 collective-permute-start.6
  791.5 190.2 %all-gather.29.cloned.1.call-start = ((), (), s32[]{:S(2)}) async-start(), calls=%async_computation.13 | async-start | bytes 2621440 | tf_op jit(solution)/shard_map/all_gather | solution.py:56
  894.9 9.2 collective-permute-start.7
  917.3 4.2 collective-permute-start.8
  930.7 13.2 copy-start.179
  930.7 13.8 copy-start.178
  930.8 14.4 copy-start.177
  930.8 15.0 copy-start.176
  930.8 15.6 copy-start.183
  930.8 16.2 copy-start.182
  930.8 16.8 copy-start.181
  930.8 17.3 copy-start.180
  934.6 16.9 copy-start.147
  934.6 16.9 copy-start.167
  934.6 16.9 copy-start.204
  934.6 203.2 %reduce-scatter.22.cloned.1.call-start = ((), (), s32[]{:S(2)}) async-start(), calls=%async_computation.17 | async-start | bytes 1114112
  951.5 14.1 copy-start.259
  951.5 14.1 copy-start.260
  981.6 204.3 %reduce-scatter.18.cloned.1.call-start = ((), (), s32[]{:S(2)}) async-start(), calls=%async_computation.15 | async-start | bytes 1253376
  1006.6 25.7 %copy-start.175 = (f32[2304]{0:T(1024)S(1)}, f32[2304]{0:T(1024)}, u32[]{:S(2)}) copy-start(f32[2304]{0:T(1024)} %get-tuple-element.988) | copy-start | bytes 27652
  1027.4 14.3 collective-permute-start.9
  1041.4 211.7 %reduce-scatter.20.cloned.1.call-start = ((), (), s32[]{:S(2)}) async-start(), calls=%async_computation.16 | async-start | bytes 557056
  1056.0 333.2 %reduce-scatter.16.cloned.1.call-start = ((), (), s32[]{:S(2)}) async-start(), calls=%async_computation.14 | async-start | bytes 1253376
  1058.4 827.0 %all-reduce.50.cloned.1.call-start = ((), (), s32[]{:S(2)}) async-start(), calls=%async_computation.18 | async-start | bytes 36700160
  1119.4 950.2 %reduce-scatter.14.cloned.1.call-start = ((), (), s32[]{:S(2)}) async-start(), calls=%async_computation.7 | async-start | bytes 8912896 | tf_op jit(solution)/shard_map/reduce_scatter | solution.py:332
  1134.7 52.7 %copy-start.252 = (f32[256]{0:T(256)S(1)}, f32[256]{0:T(256)}, u32[]{:S(2)}) copy-start(f32[256]{0:T(256)} %get-tuple-element.984) | copy-start | bytes 3076
  1134.7 52.7 %copy-start.19 = (f32[2,1,256,1024]{3,2,1,0:T(8,128)S(1)}, f32[2,1,256,1024]{3,2,1,0:T(8,128)}, u32[]{:S(2)}) copy-start(f32[2,1,256,1024]{3,2,1,0:T(8,128)} %copy-done.16) | copy-start | bytes 6291460
  1134.7 52.7 %copy-start.288 = (f32[256]{0:T(256)S(1)}, f32[256]{0:T(256)}, u32[]{:S(2)}) copy-start(f32[256]{0:T(256)} %fusion.506) | copy-start | bytes 3076
  1137.5 52.0 %copy-start.92 = (bf16[256,1024]{1,0:T(8,128)(2,1)S(1)}, bf16[256,1024]{1,0:T(8,128)(2,1)}, u32[]{:S(2)}) copy-start(bf16[256,1024]{1,0:T(8,128)(2,1)} %copy-done.91) | copy-start | bytes 1572868
  1137.5 52.0 %copy-start.94 = (bf16[1,256,1024]{2,1,0:T(8,128)(2,1)S(1)}, bf16[1,256,1024]{2,1,0:T(8,128)(2,1)}, u32[]{:S(2)}) copy-start(bf16[1,256,1024]{2,1,0:T(8,128)(2,1)} %copy-done.93) | copy-start | bytes 1572868
  (274 other events, 1337.7 us)
Sparse Core Ops, SparseCore 0:
  10.8 134.5 all-gather.14
  179.8 35.7 all-gather.18
  218.4 76.0 all-gather.16
  346.0 35.2 all-gather.20
  505.4 35.3 all-gather.22
  627.3 35.9 all-gather.24
  791.6 36.4 all-gather.26
  934.7 35.5 all-gather.28
  981.7 67.3 reduce-scatter.21
  1054.4 131.4 reduce-scatter.17
  1188.2 64.8 reduce-scatter.19
  1257.8 131.3 reduce-scatter.15
  1395.6 489.7 all-reduce.49
  1888.2 181.2 reduce-scatter.13
where the time goes:
time: 2090 us; the launch traced here: 2080 us
  waiting for transfers between devices  989 us (47%)
  matrix products  323 us (15%)
  other arithmetic  283 us (14%)
  local copies, waits for them, and re-layouts  217 us (10%)
  blocking collectives  199 us (10%)
  starting transfers between devices  37.1 us (2%)
  between operations  27.9 us (1%)
    unnamed x19, waiting for transfers between devices  710 us
    reduce_scatter x1, waiting for transfers between devices, shards(): lax.psum_scatter(d_out_w[None], ('dp', 'ctx'), scatter_dimension=1, tiled...  182 us
    dot_general x12, matrix products, state_output(): jnp.einsum('hts,hsp->htp', scores[None, :, :] * fading, scaled, precision...  128 us
    all_gather x1, blocking collectives, shards(): lax.all_gather(conv_local, ('dp', 'ctx'), axis=1, tiled=True)  58.4 us
    all_gather x1, waiting for transfers between devices, shards(): lax.all_gather(out_weight, ('dp', 'ctx'), axis=1, tiled=True)  45.2 us
    another operation x67, local copies, waits for them, and re-layouts  44.3 us
  transfers between devices with their start and end apart: 24, of which 11 were waited for; matrix products, arithmetic and copies ran while one was open for 22% of the time, Pallas kernels for 0%

commit v1 on v0

v1 whole, which is shorter than its diff:
```python
import functools

import jax
import jax.numpy as jnp
from jax import lax
from jax.experimental import pallas as pl
from jax.experimental.pallas import tpu as pltpu
from jax.sharding import PartitionSpec as P

D = 1024
E = 2048
H = 32
P_SIZE = 64
N = 128
KW = 4
CC = 2304
NPROJ = 4384

EH = E // 2
HH = H // 2
LANES = 128
CL = EH + 2 * N
COLS = EH + CL + LANES
NS = N + 16
TILE = 128
WIDE = 256
EPS = 1e-05
VMEM = 56 * 2**20
GRID = ("dp", "ctx")
f32 = jnp.float32
bf16 = jnp.bfloat16


def dot(a, b):
    return jnp.dot(a.astype(bf16), b.astype(bf16), preferred_element_type=f32)


def dot_nt(a, b):
    return lax.dot_general(
        a.astype(bf16), b.astype(bf16), (((1,), (1,)), ((), ())), preferred_element_type=f32
    )


def dot_exact(a, b):
    return jnp.dot(a, b, preferred_element_type=f32, precision=lax.Precision.HIGHEST)


def sigmoid(v):
    return 1.0 / (1.0 + jnp.exp(-v))


def softplus(v):
    return jnp.maximum(v, 0.0) + jnp.log1p(jnp.exp(-jnp.abs(v)))


def lanes_of(shape):
    return lax.broadcasted_iota(jnp.int32, shape, len(shape) - 1)


def rows_of(shape):
    return lax.broadcasted_iota(jnp.int32, shape, len(shape) - 2)


def head_columns(values, first, width):
    turned = pltpu.roll(values, lax.rem(LANES - first, LANES), 1)
    low = lanes_of((values.shape[0], LANES)) < P_SIZE
    columns = [turned[:, i : i + 1] for i in range(width // P_SIZE)]
    tiles = [
        jnp.where(low, columns[2 * i], columns[2 * i + 1]) for i in range(width // LANES)
    ]
    spread = tiles[0] if len(tiles) == 1 else jnp.concatenate(tiles, axis=1)
    return spread, columns


def chain(refs):
    total = None
    for ref in reversed(refs):
        part = ref[0, :N, :].astype(f32)
        if total is None:
            total = part
        else:
            fade = ref[0, N : N + 1, :].astype(f32) + ref[0, N + 8 : N + 9, :].astype(f32)
            total = part + fade * total
    return total


def fade_rows(row):
    high = row.astype(bf16).astype(f32)
    which = rows_of((16, row.shape[1])) < 8
    return jnp.where(which, high, row - high).astype(bf16)


def conv_rows(ext, values, edge, taps, marks):
    length = values.shape[0]
    ext[0:8, :] = edge
    ext[8 : 8 + length, :] = values.astype(bf16).astype(f32)
    summed = jnp.broadcast_to(taps[KW : KW + 1, :], values.shape)
    for k in range(KW):
        d = KW - 1 - k
        piece = ext[8 - d : 8 - d + length, :]
        if d:
            piece = piece * marks[:, d : d + 1]
        summed = summed + taps[k : k + 1, :] * piece
    return summed


def conv_back(ext, dext, d_pre, taps, marks, edge_ref, grads_ref, extra_rows):
    length = d_pre.shape[0]
    sums = []
    dext[0:8, :] = jnp.zeros((8, d_pre.shape[1]), f32)
    dext[8 : 8 + length, :] = taps[KW - 1 : KW, :] * d_pre
    for k in range(KW):
        d = KW - 1 - k
        masked = d_pre * marks[:, d : d + 1] if d else d_pre
        sums.append(jnp.sum(masked * ext[8 - d : 8 - d + length, :], axis=0, keepdims=True))
        if d:
            dext[8 - d : 8 - d + length, :] += taps[k : k + 1, :] * masked
    sums.append(jnp.sum(d_pre, axis=0, keepdims=True))
    sums += extra_rows
    sums.append(jnp.zeros((8 - len(sums), d_pre.shape[1]), f32))
    grads_ref[0] = jnp.concatenate(sums, axis=0)
    edge_ref[0] = dext[0:8, :]
    return dext[8 : 8 + length, :]


def step_parts(raw_ref, heads_ref):
    raw = raw_ref[0] + heads_ref[0:1, :]
    step = softplus(raw)
    rates = step * heads_ref[1:2, :]
    length = raw.shape[0]
    lower = (rows_of((length, length)) >= lanes_of((length, length))).astype(f32)
    return raw, step, rates, dot_exact(lower, rates)


def forward_local(
    x_ref, bc_ref, raw_ref, edge_x_ref, edge_bc_ref, marks_ref, seg_ref, taps_x_ref, taps_bc_ref,
    heads_ref, skip_ref, y_ref, state_ref, bc_out, cum_out,
    ext, ext_bc, scores, step_s, cum_s, cum_t,
):
    tile = pl.program_id(1)
    length = x_ref.shape[1]
    marks = marks_ref[0]

    @pl.when(tile == 0)
    def _():
        pre = conv_rows(ext_bc, bc_ref[0], edge_bc_ref[0], taps_bc_ref, marks)
        active = pre * sigmoid(pre)
        bc_out[0] = active
        _, step, _, cum = step_parts(raw_ref, heads_ref)
        step_s[...] = step
        cum_s[...] = cum
        cum_out[0] = cum
        cum_t[...] = cum.T
        shape = (length, length)
        keep = (rows_of(shape) >= lanes_of(shape)) & (marks[:, 7:8] == seg_ref[0, 0:1, :])
        scores[...] = jnp.where(keep, dot_nt(active[:, N:], active[:, :N]), 0.0)

    pre = conv_rows(ext, x_ref[0], edge_x_ref[0], taps_x_ref, marks)
    active = pre * sigmoid(pre)
    spread_step, _ = head_columns(step_s[...], 2 * tile, TILE)
    spread_cum, columns = head_columns(cum_s[...], 2 * tile, TILE)
    last = spread_cum[length - 1 : length, :]
    scaled = active * spread_step
    end = scaled * (jnp.exp(last - spread_cum) * marks[:, 5:6])
    writer = bc_out[0, :, :N]
    state_ref[0, :N, :] = dot(writer.T, end).astype(bf16)
    state_ref[0, N:, :] = fade_rows(jnp.exp(last) * marks[0:1, 6:7])
    outs = []
    for i in range(2):
        row = cum_t[pl.ds(2 * tile + i, 1), :]
        fade = jnp.exp(jnp.minimum(columns[i] - row, 0.0))
        outs.append(dot(scores[...] * fade, scaled[:, i * P_SIZE : (i + 1) * P_SIZE]))
    y_ref[0] = jnp.concatenate(outs, axis=1) + skip_ref[0:1, :] * active


def forward_join(hops, *refs):
    states = refs[:hops]
    (y_ref, gate_ref, bc_ref, cum_ref, marks_ref, gain_ref, wout_ref, mixed_ref, mem_ref, part_ref,
     total) = refs[hops:]
    tile = pl.program_id(1)
    tiles = pl.num_programs(1)
    marks = marks_ref[0]
    memory = chain(states)
    mem_ref[0] = memory.astype(bf16)
    carry, _ = head_columns(jnp.exp(cum_ref[0]) * marks[:, 4:5], (WIDE // P_SIZE) * tile, WIDE)
    mixed = y_ref[0] + carry * dot(bc_ref[0, :, N:], memory)
    mixed_ref[0] = mixed
    gate = gate_ref[0]
    gated = mixed * gate * sigmoid(gate)
    part = dot(gated * gain_ref[0:1, :], wout_ref[...])
    stat = jnp.sum(gated * gated, axis=1, keepdims=True)

    @pl.when(tile == 0)
    def _():
        total[:, :D] = part
        total[:, D:] = jnp.broadcast_to(stat, (stat.shape[0], LANES))

    @pl.when(tile > 0)
    def _():
        total[:, :D] += part
        total[:, D:] += jnp.broadcast_to(stat, (stat.shape[0], LANES))

    @pl.when(tile == tiles - 1)
    def _():
        part_ref[0] = total[...]


def backward_gate(
    grad_ref, wout_ref, total_ref, mixed_ref, gate_ref, bc_ref, cum_ref, marks_ref, gain_ref,
    dy_ref, dgate_ref, normed_ref, gain_grad_ref, state_ref, moment,
):
    tile = pl.program_id(1)
    length = grad_ref.shape[1]
    marks = marks_ref[0]

    @pl.when(tile == 0)
    def _():
        inner = jnp.sum(grad_ref[0].astype(f32) * total_ref[0, :, :D], axis=1, keepdims=True)
        moment[...] = jnp.broadcast_to(inner / E, (length, LANES))

    scale = lax.rsqrt(total_ref[0, :, D : D + 1] / E + EPS)
    d_normed = dot_nt(grad_ref[0], wout_ref[...])
    gate = gate_ref[0]
    sig = sigmoid(gate)
    silu = gate * sig
    mixed = mixed_ref[0]
    gated = mixed * silu
    gain = gain_ref[0:1, :]
    normed_ref[0] = (gated * scale * gain).astype(bf16)
    gain_grad_ref[0] = jnp.broadcast_to(
        jnp.sum(d_normed * gated * scale, axis=0, keepdims=True), (8, WIDE)
    )
    d_gated = scale * (gain * d_normed) - gated * (scale * scale * scale * moment[:, 0:1])
    dy = d_gated * silu
    dy_ref[0] = dy
    dgate_ref[0] = (d_gated * mixed * (sig + silu * (1.0 - sig))).astype(bf16)
    spread, _ = head_columns(cum_ref[0], (WIDE // P_SIZE) * tile, WIDE)
    carry = jnp.exp(spread) * marks[:, 4:5]
    state_ref[0, :N, :] = dot(bc_ref[0, :, N:].T, dy * carry).astype(bf16)
    last = spread[length - 1 : length, :]
    state_ref[0, N:, :] = fade_rows(jnp.exp(last) * marks[0:1, 6:7])


def backward_local(hops, *refs):
    states = refs[:hops]
    (x_ref, bc_ref, raw_ref, edge_x_ref, edge_bc_ref, marks_ref, seg_ref, taps_x_ref, taps_bc_ref,
     heads_ref, skip_ref, dy_ref, mixed_ref, mem_ref,
     dx_ref, dbc_ref, draw_ref, edge_x_out, edge_bc_out, grads_x_ref, grads_bc_ref, grads_h_ref,
     ext, dext, ext_bc, dext_bc, pre_bc, active_bc, scores, d_scores, raw_s, step_s, rates_s, cum_s,
     cum_t, d_bc, d_cum, d_step) = refs[hops:]
    tile = pl.program_id(1)
    tiles = pl.num_programs(1)
    length = x_ref.shape[1]
    marks = marks_ref[0]
    shape = (length, length)
    keep = (rows_of(shape) <= lanes_of(shape)) & (marks[:, 7:8] == seg_ref[0, 0:1, :])

    @pl.when(tile == 0)
    def _():
        pre = conv_rows(ext_bc, bc_ref[0], edge_bc_ref[0], taps_bc_ref, marks)
        active = pre * sigmoid(pre)
        pre_bc[...] = pre
        active_bc[...] = active
        raw, step, rates, cum = step_parts(raw_ref, heads_ref)
        raw_s[...] = raw
        step_s[...] = step
        rates_s[...] = rates
        cum_s[...] = cum
        cum_t[...] = cum.T
        scores[...] = jnp.where(keep, dot_nt(active[:, :N], active[:, N:]), 0.0)
        d_scores[...] = jnp.zeros(shape, f32)
        d_bc[...] = jnp.zeros((length, 2 * N), f32)
        d_cum[...] = jnp.zeros((length, LANES), f32)
        d_step[...] = jnp.zeros((length, LANES), f32)

    pre = conv_rows(ext, x_ref[0], edge_x_ref[0], taps_x_ref, marks)
    sig = sigmoid(pre)
    active = pre * sig
    spread_step, _ = head_columns(step_s[...], 2 * tile, TILE)
    spread_cum, columns = head_columns(cum_s[...], 2 * tile, TILE)
    last = spread_cum[length - 1 : length, :]
    scaled = active * spread_step
    end_weight = jnp.exp(last - spread_cum) * marks[:, 5:6]
    carry = jnp.exp(spread_cum) * marks[:, 4:5]
    end = scaled * end_weight
    through = jnp.exp(last) * marks[0:1, 6:7]
    later = chain(states)
    memory = mem_ref[0].astype(f32)
    writer = active_bc[:, :N]
    dy = dy_ref[0]
    back = dot(writer, later)
    d_bc[:, :N] += dot_nt(end, later)
    d_bc[:, N:] += dot_nt(dy * carry, memory)
    d_scaled = []
    total_scores = d_scores[...]
    for i in range(2):
        cut = slice(i * P_SIZE, (i + 1) * P_SIZE)
        row = cum_t[pl.ds(2 * tile + i, 1), :]
        fade = jnp.exp(jnp.minimum(row - columns[i], 0.0))
        total_scores = total_scores + dot_nt(scaled[:, cut], dy[:, cut]) * fade
        d_scaled.append(dot(scores[...] * fade, dy[:, cut]))
    d_scores[...] = total_scores
    d_diag = jnp.concatenate(d_scaled, axis=1)
    skip = skip_ref[0:1, :]
    rounded_dy = dy.astype(bf16).astype(f32)
    rounded_scaled = scaled.astype(bf16).astype(f32)
    ended = end * back
    gaps = rounded_dy * (mixed_ref[0] - skip * active) - rounded_scaled * d_diag - ended
    closing = jnp.sum(ended, axis=0, keepdims=True) + through * jnp.sum(
        later * memory, axis=0, keepdims=True
    )
    gaps = gaps + jnp.where(rows_of((length, LANES)) == length - 1, closing, 0.0)
    d_all = d_diag + end_weight * back
    places = (
        lax.broadcasted_iota(jnp.int32, (LANES, LANES), 1)
        == 2 * tile + (lax.broadcasted_iota(jnp.int32, (LANES, LANES), 0) >= P_SIZE).astype(jnp.int32)
    ).astype(bf16)
    places = jnp.concatenate([places, places], axis=0)

    def per_head(values):
        high = values.astype(bf16)
        rest = (values - high.astype(f32)).astype(bf16)
        return jnp.dot(
            jnp.concatenate([high, rest], axis=1), places, preferred_element_type=f32
        )

    d_cum[...] += per_head(gaps)
    d_step[...] += per_head(d_all * active)
    d_active = d_all * spread_step + skip * dy
    d_pre = d_active * (sig + active * (1.0 - sig))
    dx_ref[0] = conv_back(
        ext, dext, d_pre, taps_x_ref, marks, edge_x_out, grads_x_ref,
        [jnp.sum(dy * active, axis=0, keepdims=True)],
    )

    @pl.when(tile == tiles - 1)
    def _():
        reader = active_bc[:, N:]
        kept = jnp.where(keep, d_scores[...], 0.0)
        d_bc[:, :N] += dot(kept, reader)
        d_bc[:, N:] += dot(kept.T, active_bc[:, :N])
        pre2 = pre_bc[...]
        sig2 = sigmoid(pre2)
        d_pre2 = d_bc[...] * (sig2 + pre2 * sig2 * (1.0 - sig2))
        dbc_ref[0] = conv_back(
            ext_bc, dext_bc, d_pre2, taps_bc_ref, marks, edge_bc_out, grads_bc_ref, []
        )
        upper = (rows_of(shape) <= lanes_of(shape)).astype(f32)
        d_rates = dot_exact(upper, d_cum[...])
        d_raw = (d_step[...] + d_rates * heads_ref[1:2, :]) * sigmoid(raw_s[...])
        draw_ref[0] = d_raw
        grads_h_ref[0] = jnp.concatenate(
            [
                jnp.sum(d_raw, axis=0, keepdims=True),
                jnp.sum(d_rates * rates_s[...], axis=0, keepdims=True),
                jnp.zeros((6, LANES), f32),
            ],
            axis=0,
        )


def backward_project(
    dgate_ref, dx_ref, dbc_ref, draw_ref, edge_ref, win_ref, dproj_ref, dn_ref, held
):
    length = dx_ref.shape[1]
    held[:, :EH] = dx_ref[0]
    held[:, EH:] = dbc_ref[0]
    held[length - 8 :, :] += edge_ref[0]
    dproj_ref[0, :, :EH] = dgate_ref[0]
    dproj_ref[0, :, EH : EH + CL] = held[...].astype(bf16)
    dproj_ref[0, :, EH + CL :] = draw_ref[0].astype(bf16)
    dn_ref[0] = dot_nt(dproj_ref[0], win_ref[...])


def spec(block, index):
    return pl.BlockSpec(block, index)


def params():
    return pltpu.CompilerParams(vmem_limit_bytes=VMEM)


def row_tile(length, width, first=0):
    return spec((1, length, width), lambda r, t: (r, 0, first + t))


def row_fixed(length, width, column=0):
    return spec((1, length, width), lambda r, t: (r, 0, column))


def flat_tile(rows, width):
    return spec((rows, width), lambda r, t: (0, t))


def flat_fixed(rows, width):
    return spec((rows, width), lambda r, t: (0, 0))


def out(*shape, dtype=f32):
    return jax.ShapeDtypeStruct(shape, dtype)


def cost(flops, moved):
    return pl.CostEstimate(flops=int(flops), bytes_accessed=int(moved), transcendentals=0)


def local_specs(length):
    return [
        row_tile(length, TILE, EH // TILE),
        row_fixed(length, 2 * N, 2 * EH // (2 * N)),
        row_fixed(length, LANES, (EH + CL) // LANES),
        row_tile(8, TILE),
        row_fixed(8, 2 * N, EH // (2 * N)),
        row_fixed(length, LANES),
        row_fixed(8, length),
        flat_tile(8, TILE),
        spec((8, 2 * N), lambda r, t: (0, EH // (2 * N))),
        flat_fixed(8, LANES),
        flat_tile(8, TILE),
    ]


def run_forward_local(proj, edge, marks, seg_rows, layer):
    rows, length, _ = proj.shape
    return pl.pallas_call(
        forward_local,
        grid=(rows, EH // TILE),
        in_specs=local_specs(length),
        out_specs=[
            row_tile(length, TILE), row_tile(NS, TILE), row_fixed(length, 2 * N),
            row_fixed(length, LANES),
        ],
        out_shape=[
            out(rows, length, EH), out(rows, NS, EH, dtype=bf16), out(rows, length, 2 * N),
            out(rows, length, LANES),
        ],
        scratch_shapes=[
            pltpu.VMEM((length + 8, TILE), f32), pltpu.VMEM((length + 8, 2 * N), f32),
            pltpu.VMEM((length, length), f32), pltpu.VMEM((length, LANES), f32),
            pltpu.VMEM((length, LANES), f32), pltpu.VMEM((LANES, length), f32),
        ],
        compiler_params=params(),
        cost_estimate=cost(rows * length * length * EH * 2 * 16, rows * length * EH * 12),
        name="forward_local",
    )(proj, proj, proj, edge, edge, marks, seg_rows, layer["taps"], layer["taps"], layer["heads"],
      layer["skip"])


def run_forward_join(states, y, proj, bc, cum, marks, gain, wout):
    rows, length, _ = y.shape
    hops = len(states)
    return pl.pallas_call(
        functools.partial(forward_join, hops),
        grid=(rows, EH // WIDE),
        in_specs=[row_tile(NS, WIDE)] * hops + [
            row_tile(length, WIDE), row_tile(length, WIDE), row_fixed(length, 2 * N),
            row_fixed(length, LANES), row_fixed(length, LANES), flat_tile(8, WIDE),
            spec((WIDE, D), lambda r, t: (t, 0)),
        ],
        out_specs=[
            row_tile(length, WIDE), row_tile(N, WIDE), row_fixed(length, D + LANES),
        ],
        out_shape=[
            out(rows, length, EH), out(rows, N, EH, dtype=bf16), out(rows, length, D + LANES),
        ],
        scratch_shapes=[pltpu.VMEM((length, D + LANES), f32)],
        compiler_params=params(),
        name="forward_join",
    )(*states, y, proj, bc, cum, marks, gain, wout)


def run_backward_gate(grad, wout, total, mixed, proj, bc, cum, marks, gain):
    rows, length, _ = mixed.shape
    return pl.pallas_call(
        backward_gate,
        grid=(rows, EH // WIDE),
        in_specs=[
            row_fixed(length, D), spec((WIDE, D), lambda r, t: (t, 0)),
            row_fixed(length, D + LANES), row_tile(length, WIDE), row_tile(length, WIDE),
            row_fixed(length, 2 * N), row_fixed(length, LANES), row_fixed(length, LANES),
            flat_tile(8, WIDE),
        ],
        out_specs=[
            row_tile(length, WIDE), row_tile(length, WIDE), row_tile(length, WIDE),
            row_tile(8, WIDE), row_tile(NS, WIDE),
        ],
        out_shape=[
            out(rows, length, EH), out(rows, length, EH, dtype=bf16),
            out(rows, length, EH, dtype=bf16), out(rows, 8, EH), out(rows, NS, EH, dtype=bf16),
        ],
        scratch_shapes=[pltpu.VMEM((length, LANES), f32)],
        compiler_params=params(),
        name="backward_gate",
    )(grad, wout, total, mixed, proj, bc, cum, marks, gain)


def run_backward_local(states, proj, edge, marks, seg_rows, layer, dy, mixed, memory):
    rows, length, _ = proj.shape
    hops = len(states)
    tall = lambda width: pltpu.VMEM((length + 8, width), f32)
    flat = lambda width: pltpu.VMEM((length, width), f32)
    return pl.pallas_call(
        functools.partial(backward_local, hops),
        grid=(rows, EH // TILE),
        in_specs=[row_tile(NS, TILE)] * hops + local_specs(length) + [
            row_tile(length, TILE), row_tile(length, TILE), row_tile(N, TILE),
        ],
        out_specs=[
            row_tile(length, TILE), row_fixed(length, 2 * N), row_fixed(length, LANES),
            row_tile(8, TILE), row_fixed(8, 2 * N), row_tile(8, TILE), row_fixed(8, 2 * N),
            row_fixed(8, LANES),
        ],
        out_shape=[
            out(rows, length, EH), out(rows, length, 2 * N), out(rows, length, LANES),
            out(rows, 8, EH), out(rows, 8, 2 * N), out(rows, 8, EH), out(rows, 8, 2 * N),
            out(rows, 8, LANES),
        ],
        scratch_shapes=[
            tall(TILE), tall(TILE), tall(2 * N), tall(2 * N), flat(2 * N), flat(2 * N),
            flat(length), flat(length), flat(LANES), flat(LANES), flat(LANES), flat(LANES),
            pltpu.VMEM((LANES, length), f32), flat(2 * N), flat(LANES), flat(LANES),
        ],
        compiler_params=params(),
        name="backward_local",
    )(*states, proj, proj, proj, edge, edge, marks, seg_rows, layer["taps"], layer["taps"],
      layer["heads"], layer["skip"], dy, mixed, memory)


def run_backward_project(dgate, dx, dbc, draw, edge, win):
    rows, length, _ = dx.shape
    block = lambda width: spec((1, length, width), lambda r: (r, 0, 0))
    return pl.pallas_call(
        backward_project,
        grid=(rows,),
        in_specs=[
            block(EH), block(EH), block(2 * N), block(LANES),
            spec((1, 8, CL), lambda r: (r, 0, 0)), spec((D, COLS), lambda r: (0, 0)),
        ],
        out_specs=[block(COLS), block(D)],
        out_shape=[out(rows, length, COLS, dtype=bf16), out(rows, length, D)],
        scratch_shapes=[pltpu.VMEM((length, CL), f32)],
        compiler_params=params(),
        name="backward_project",
    )(dgate, dx, dbc, draw, edge, win)


def shifted(values, axis, by):
    length = lax.axis_size(axis)
    pairs = [(i, i + by) for i in range(length) if 0 <= i + by < length]
    return lax.ppermute(values, axis, pairs)


def swapped(values):
    return lax.ppermute(values, "section", [(0, 1), (1, 0)])


def summed_over(values, axis):
    step = 1
    size = lax.axis_size(axis)
    while step < size:
        values = values + lax.ppermute(values, axis, [(i, i ^ step) for i in range(size)])
        step *= 2
    return values


def gathered(shard):
    return lax.all_gather(shard, GRID, axis=0, tiled=True)


def scattered(values):
    return lax.psum_scatter(values, GRID, scatter_dimension=0, tiled=True)


def of_core(values, core, axis, size):
    shape = values.shape
    split = values.reshape(shape[:axis] + (shape[axis] // (2 * size), 2, size) + shape[axis + 1 :])
    taken = lax.dynamic_index_in_dim(split, core, axis + 1, False)
    return taken.reshape(shape[:axis] + (shape[axis] // 2,) + shape[axis + 1 :])


def interleaved(even, odd, axis, size):
    shape = even.shape
    split = shape[:axis] + (shape[axis] // size, size) + shape[axis + 1 :]
    both = jnp.stack([even.reshape(split), odd.reshape(split)], axis=axis + 1)
    return both.reshape(shape[:axis] + (2 * shape[axis],) + shape[axis + 1 :])


def in_half(weight, core):
    rows = weight.shape[0]
    return jnp.concatenate(
        [
            of_core(weight[:, :E], core, 1, P_SIZE),
            of_core(weight[:, E : 2 * E], core, 1, P_SIZE),
            weight[:, 2 * E : 2 * E + 2 * N],
            of_core(weight[:, E + CC :], core, 1, 1),
            jnp.zeros((rows, LANES - HH), weight.dtype),
        ],
        axis=1,
    )


def shards(
    hidden, cotangent, segments, in_weight, out_weight, conv_weight, conv_bias, norm_gain,
    gate_gain, step_bias, decay_log, skip_gain,
):
    core = lax.axis_index("section")
    ctx_id = lax.axis_index("ctx")
    ctx_size = lax.axis_size("ctx")
    batches, rows_here, length, _ = hidden.shape
    rows = batches * rows_here
    is_first = core == 0
    by_layer = lambda own, other: (
        jnp.where(is_first, own, other), jnp.where(is_first, other, own)
    )

    whole_heads = out_weight.shape[1] % (2 * P_SIZE) == 0
    own_in = in_half(in_weight[0], core)
    other_in = swapped(in_half(in_weight[0], 1 - core))
    win = [gathered(part) for part in by_layer(own_in, other_in)]
    out_rows = out_weight[0] if whole_heads else gathered(out_weight[0])
    own_out = of_core(out_rows, core, 0, P_SIZE)
    other_out = swapped(of_core(out_rows, 1 - core, 0, P_SIZE))
    wout = by_layer(own_out, other_out)
    if whole_heads:
        wout = [gathered(part) for part in wout]

    channels = conv_bias.shape[1]
    pack = jnp.concatenate(
        [
            conv_weight[0].reshape(-1), conv_bias[0], norm_gain[0], gate_gain[0],
        ]
    ).astype(f32)
    heads_own = jnp.concatenate([step_bias[0], decay_log[0], skip_gain[0]])
    everything = lax.all_gather(
        jnp.concatenate([pack, heads_own])[None], ("section",) + GRID, axis=0, tiled=True
    ).reshape(2, -1, pack.shape[0] + 3 * H)
    d_share, e_share = norm_gain.shape[1], gate_gain.shape[1]

    def layer_params(l):
        part = everything[l]
        taps = part[:, : KW * channels].reshape(-1, KW, channels).swapaxes(0, 1).reshape(KW, CC)
        at = KW * channels
        bias = part[:, at : at + channels].reshape(1, CC)
        gain_in = part[:, at + channels : at + channels + d_share].reshape(D)
        at = at + channels + d_share
        gain_gate = part[:, at : at + e_share].reshape(E)
        per_head = part[0, at + e_share :].reshape(3, H)
        taps = jnp.concatenate([taps, bias, jnp.zeros((3, CC), f32)], axis=0)
        taps = jnp.concatenate([of_core(taps[:, :E], core, 1, P_SIZE), taps[:, E:]], axis=1)
        per_head = of_core(per_head, core, 1, 1)
        rates = -jnp.exp(per_head[1])
        heads = jnp.zeros((8, LANES), f32)
        heads = heads.at[0, :HH].set(per_head[0]).at[1, :HH].set(rates)
        skip = jnp.broadcast_to(jnp.repeat(per_head[2], P_SIZE)[None], (8, EH))
        gain = jnp.broadcast_to(of_core(gain_gate, core, 0, P_SIZE)[None], (8, EH))
        return {"taps": taps, "heads": heads, "skip": skip, "gain": gain, "norm": gain_in}

    layers = [layer_params(0), layer_params(1)]

    lead = jnp.full((batches, rows_here, KW - 1), -1, jnp.int32)
    seg_ext = lax.dynamic_slice_in_dim(
        jnp.concatenate([lead, segments], axis=2), ctx_id * length, length + KW - 1, 2
    ).reshape(rows, length + KW - 1)
    seg = seg_ext[:, KW - 1 :]
    before = seg_ext[:, KW - 2 : KW - 1]
    final = seg[:, -1:]
    columns = [
        (seg_ext[:, KW - 1 - d : KW - 1 - d + length] == seg).astype(f32) for d in range(KW)
    ]
    columns += [
        (seg == before).astype(f32), (seg == final).astype(f32),
        jnp.broadcast_to((final == before).astype(f32), seg.shape), seg.astype(f32),
    ]
    marks = jnp.stack(columns + [jnp.zeros(seg.shape, f32)] * (LANES - len(columns)), axis=-1)
    seg_rows = jnp.broadcast_to(seg.astype(f32)[:, None, :], (rows, 8, length))

    def forward(u, l):
        layer = layers[l]
        scale = lax.rsqrt(jnp.mean(u * u, axis=-1, keepdims=True) + EPS)
        normed = (u * scale * layer["norm"]).astype(bf16)
        proj = jnp.dot(
            normed.reshape(-1, D), win[l], preferred_element_type=f32
        ).reshape(rows, length, COLS)
        tail = proj[:, length - 8 :, EH : EH + CL].astype(bf16)
        edge = shifted(tail, "ctx", 1).astype(f32)
        y, state, bc, cum = run_forward_local(proj, edge, marks, seg_rows, layer)
        arrived = [shifted(state, "ctx", k) for k in range(1, ctx_size)]
        mixed, memory, part = run_forward_join(
            arrived, y, proj, bc, cum, marks, layer["gain"], wout[l]
        )
        total = part + swapped(part)
        branch = lax.rsqrt(total[:, :, D : D + 1] / E + EPS) * total[:, :, :D]
        kept = (u, normed, proj, edge, bc, cum, mixed, memory, total)
        return (u + branch).astype(bf16), kept

    def backward(g, l, kept):
        u, normed, proj, edge, bc, cum, mixed, memory, total = kept
        layer = layers[l]
        low = g.astype(bf16)
        dy, dgate, normed_out, gain_grad, state = run_backward_gate(
            low, wout[l], total, mixed, proj, bc, cum, marks, layer["gain"]
        )
        arrived = [shifted(state, "ctx", -k) for k in range(1, ctx_size)]
        d_wout = lax.dot_general(
            normed_out.reshape(-1, EH), low.reshape(-1, D), (((0,), (0,)), ((), ())),
            preferred_element_type=f32,
        ).astype(bf16)
        dx, dbc, draw, edge_x, edge_bc, grads_x, grads_bc, grads_h = run_backward_local(
            arrived, proj, edge, marks, seg_rows, layer, dy, mixed, memory
        )
        edge_back = shifted(jnp.concatenate([edge_x, edge_bc], axis=2), "ctx", -1)
        dproj, dn = run_backward_project(dgate, dx, dbc, draw, edge_back, win[l])
        d_win = lax.dot_general(
            normed.reshape(-1, D), dproj.reshape(-1, COLS), (((0,), (0,)), ((), ())),
            preferred_element_type=f32,
        ).astype(bf16)
        dn = dn + swapped(dn)
        scale = lax.rsqrt(jnp.mean(u * u, axis=-1, keepdims=True) + EPS)
        gained = layer["norm"] * dn
        d_u = g + scale * gained - u * scale**3 * jnp.mean(u * gained, axis=-1, keepdims=True)
        d_norm = jnp.sum(dn * u * scale, axis=(0, 1))
        sums_x = jnp.sum(grads_x, axis=0)
        sums_h = jnp.sum(grads_h, axis=0)
        small = jnp.concatenate(
            [
                sums_x[: KW + 1].reshape(-1),
                jnp.sum(grads_bc, axis=0)[: KW + 1].reshape(-1),
                jnp.sum(gain_grad, axis=0)[0],
                d_norm,
                sums_h[0, :HH],
                sums_h[1, :HH],
                jnp.sum(sums_x[KW + 1].reshape(HH, P_SIZE), axis=1),
            ]
        )
        return d_u.astype(bf16), d_win, d_wout, small

    source = hidden.reshape(rows, length, D).astype(f32)
    one, kept_one = forward(source, 0)
    two, kept_two = forward(one.astype(f32), 1)
    goal = cotangent.reshape(rows, length, D).astype(f32)
    d_two, d_win_two, d_wout_two, small_two = backward(goal, 1, kept_two)
    d_one, d_win_one, d_wout_one, small_one = backward(d_two.astype(f32), 0, kept_one)

    def owned(first, second):
        mine = jnp.where(is_first, first, second)
        arrived = swapped(jnp.where(is_first, second, first))
        even, odd = by_layer(mine, arrived)
        return mine, arrived, even, odd

    mine, arrived, even, odd = owned(scattered(d_win_one), scattered(d_win_two))
    both = mine[:, 2 * EH : 2 * EH + 2 * N].astype(f32) + arrived[
        :, 2 * EH : 2 * EH + 2 * N
    ].astype(f32)
    at = EH + CL
    in_grad = jnp.concatenate(
        [
            interleaved(even[:, : 2 * EH], odd[:, : 2 * EH], 1, P_SIZE).astype(f32),
            both,
            interleaved(even[:, at : at + HH], odd[:, at : at + HH], 1, 1).astype(f32),
        ],
        axis=1,
    )
    if whole_heads:
        mine, arrived, even, odd = owned(scattered(d_wout_one), scattered(d_wout_two))
        out_grad = interleaved(even, odd, 0, P_SIZE).astype(f32)
    else:
        spread = lambda part: scattered(
            interleaved(*by_layer(part, jnp.zeros_like(part)), 0, P_SIZE)
        )
        mine, arrived, even, odd = owned(spread(d_wout_one), spread(d_wout_two))
        out_grad = mine.astype(f32) + arrived.astype(f32)

    small = jnp.stack([small_one, small_two])
    small = summed_over(summed_over(small, "ctx"), "dp")
    mine, arrived, even, odd = owned(small[0], small[1])
    place = lax.axis_index("dp") * ctx_size + ctx_id
    size = (KW + 1) * EH
    conv_x = interleaved(even[:size].reshape(KW + 1, EH), odd[:size].reshape(KW + 1, EH), 1, P_SIZE)
    conv_bc = (mine + arrived)[size : size + (KW + 1) * 2 * N].reshape(KW + 1, 2 * N)
    conv_all = lax.dynamic_slice_in_dim(
        jnp.concatenate([conv_x, conv_bc], axis=1), place * channels, channels, 1
    )
    size += (KW + 1) * 2 * N
    gate_all = interleaved(even[size : size + EH], odd[size : size + EH], 0, P_SIZE)
    size += EH
    norm_all = mine[size : size + D]
    size += D
    per_head = [
        interleaved(even[size + i * HH : size + (i + 1) * HH], odd[size + i * HH : size + (i + 1) * HH], 0, 1)
        for i in range(3)
    ]
    own_shape = (1, batches, rows_here, length, D)
    return (
        jnp.where(is_first, one, two).reshape(own_shape),
        jnp.where(is_first, d_one, d_two).reshape(own_shape),
        in_grad[None],
        out_grad[None],
        conv_all[None, :KW],
        conv_all[None, KW],
        lax.dynamic_slice_in_dim(norm_all, place * d_share, d_share, 0)[None],
        lax.dynamic_slice_in_dim(gate_all, place * e_share, e_share, 0)[None],
        per_head[0][None],
        per_head[1][None],
        per_head[2][None],
    )


def solution(mesh):
    in_specs = (
        P(None, "dp", "ctx", None),
        P(None, "dp", "ctx", None),
        P(None, "dp", None),
        P("section", ("dp", "ctx"), None),
        P("section", ("dp", "ctx"), None),
        P("section", None, ("dp", "ctx")),
        P("section", ("dp", "ctx")),
        P("section", ("dp", "ctx")),
        P("section", ("dp", "ctx")),
        P("section", None),
        P("section", None),
        P("section", None),
    )
    out_specs = (
        P("section", None, "dp", "ctx", None),
        P("section", None, "dp", "ctx", None),
        P("section", ("dp", "ctx"), None),
        P("section", ("dp", "ctx"), None),
        P("section", None, ("dp", "ctx")),
        P("section", ("dp", "ctx")),
        P("section", ("dp", "ctx")),
        P("section", ("dp", "ctx")),
        P("section", None),
        P("section", None),
        P("section", None),
    )
    return jax.shard_map(shards, mesh=mesh, in_specs=in_specs, out_specs=out_specs, check_vma=False)
```

time: 2090 us -> 850 us (0.41)
  waiting for transfers between devices: 989 us -> 456 us
  matrix products: 323 us -> 31.4 us
  other arithmetic: 283 us -> 35.5 us
  blocking collectives: 199 us -> 0 us
  local copies, waits for them, and re-layouts: 217 us -> 49.9 us
  Pallas kernels: 0 us -> 153 us
  starting transfers between devices: 37.1 us -> 98.1 us
    unnamed x19 -> x10, waiting for transfers between devices: 710 us -> 150 us
    dot_general x59 -> x6, matrix products: 323 us -> 31.4 us  [the longest x2 13.3 us: backward(): lax.dot_general(normed.reshape(-1, D), dproj.reshape(-1, COLS), (((0,), (...]
    pallas_call x0 -> x10, Pallas kernels: none -> 153 us  [the longest x2 54.3 us: run_backward_local(): pl.pallas_call(functools.partial(backward_local, hops), grid=(rows, EH //...]
    all_gather x8 -> x0, blocking collectives: 137 us -> none  [the longest x1 58.4 us: shards(): lax.all_gather(conv_local, ('dp', 'ctx'), axis=1, tiled=True)]
    ppermute x10 -> x29, waiting for transfers between devices: 3.84 us -> 137 us  [the longest x16 107 us: shifted(): return lax.ppermute(values, axis, pairs)]
    all_gather x8 -> x4, waiting for transfers between devices: 93.7 us -> 21.7 us  [gathered(): return lax.all_gather(shard, GRID, axis=0, tiled=True)]
    ppermute x10 -> x29, starting transfers between devices: 35.8 us -> 97 us  [the longest x16 91.7 us: shifted(): return lax.ppermute(values, axis, pairs)]
    mul x37 -> x0, other arithmetic: 57.6 us -> none  [the longest x4 26.4 us: conv_state(): active = jax.nn.silu(summed)]
  transfers between devices with their start and end apart: 24 -> 38, of which waited for: 11 -> 25; matrix products, arithmetic and copies ran while one was open for 22% -> 10% of each run, Pallas kernels for 0% -> 15%
where the time goes in v1:
time: 850 us; the launch traced here: 841 us
  waiting for transfers between devices  456 us (54%)
  Pallas kernels  153 us (18%)
  starting transfers between devices  98.1 us (12%)
  local copies, waits for them, and re-layouts  49.9 us (6%)
  other arithmetic  35.5 us (4%)
  matrix products  31.4 us (4%)
  between operations  17.4 us (2%)
    unnamed x10, waiting for transfers between devices  150 us
    reduce_scatter x4, waiting for transfers between devices, scattered(): return lax.psum_scatter(values, GRID, scatter_dimension=0, tiled=True)  147 us
    ppermute x16, waiting for transfers between devices, shifted(): return lax.ppermute(values, axis, pairs)  107 us
    ppermute x16, starting transfers between devices, shifted(): return lax.ppermute(values, axis, pairs)  91.7 us
    pallas_call x2, Pallas kernels, run_backward_local(): pl.pallas_call(functools.partial(backward_local, hops), grid=(rows, EH //...  54.3 us
    pallas_call x2, Pallas kernels, run_forward_local(): pl.pallas_call(forward_local, grid=(rows, EH // TILE), in_specs=local_spe...  37.4 us
    pallas_call x2, Pallas kernels, run_forward_join(): pl.pallas_call(functools.partial(forward_join, hops), grid=(rows, EH // W...  23 us
    pallas_call x2, Pallas kernels, run_backward_gate(): pl.pallas_call(backward_gate, grid=(rows, EH // WIDE), in_specs=[row_fixe...  22.3 us
  transfers between devices with their start and end apart: 38, of which 25 were waited for; matrix products, arithmetic and copies ran while one was open for 10% of the time, Pallas kernels for 15%

profile of v1, /device:TPU:10, one launch (start us, length us, event | category | flops | bytes accessed | tf_op | source)
XLA Modules:
  0.0 840.6 jit_solution(11115823914727604444)
XLA Ops:
  11.7 6.8 dynamic-slice_reduce_fusion
  30.2 2.6 stack.97.marks_ref.refs_7_.refs_8_
  33.7 149.5 %all-reduce.6.cloned.1.call-done = f32[32256]{0:T(1024)} async-done(((f32[32256]{0:T(1024)}), f32[32256]{0:T(1024)}) %all-reduce.6.cloned.1.call-update) | async-done | bytes 129040
  187.2 5.0 fusion.2.x_ref.bc_ref.raw_ref.refs_4_.gate_ref.refs_3_.refs_5_
  192.3 2.2 copy-done
  194.5 3.6 collective-permute-start.1
  199.3 1.7 collective-permute-done.1
  202.8 18.7 %forward_local.2 = (f32[2,256,1024]{2,1,0:T(8,128)}, bf16[2,144,1024]{2,1,0:T(8,128)(2,1)}, f32[2,256,256]{2,1,0:T(8,128)}, f32[2,256,128]{2,1,0:T(8,128)}) custom-call(f32[2,256,2432]{2,1,0:T(8,128)} %copy-done, f32[2,256,2432]{2,1,0:T(8,128)} %copy-done, f32[2,256,2432]{2,1,0:T(8,128)} %copy-done, ...), custom_call_target="tpu_custom_call" | custom-call | flops 4294967296 | bytes 6291456 | tf_op jit(solution)/shard_map/forward_local/pallas_call | solution.py:425
  221.5 4.6 collective-permute-start.2
  226.1 1.3 collective-permute-start.3
  229.1 23.3 %collective-permute-done.2.refs_0_ = bf16[2,144,1024]{2,1,0:T(8,128)(2,1)S(1)} collective-permute-done((bf16[2,144,1024]{2,1,0:T(8,128)(2,1)}, bf16[2,144,1024]{2,1,0:T(8,128)(2,1)S(1)}, u32[]{:S(2)}, u32[]{:S(2)}) %collective-permute-start.2) | collective-permute-done | bytes 589856 | tf_op jit(solution)/shard_map/ppermute | solution.py:550
  252.4 3.2 collective-permute-done.3.refs_1_
  256.6 11.5 %forward_join.2 = (f32[2,256,1024]{2,1,0:T(8,128)}, bf16[2,128,1024]{2,1,0:T(8,128)(2,1)}, f32[2,256,1152]{2,1,0:T(8,128)}) custom-call(bf16[2,144,1024]{2,1,0:T(8,128)(2,1)} %copy-done.14, bf16[2,144,1024]{2,1,0:T(8,128)(2,1)} %copy-done.15, bf16[2,144,1024]{2,1,0:T(8,128)(2,1)} %copy-done.16, f32[2,256,1024]{2,1,0:T(8,128)} %get-tuple-element.104.refs_3_, ...), custom_call_target="tpu_custom_call" | custom-call | tf_op jit(solution)/shard_map/forward_join/pallas_call | solution.py:452
  269.7 3.2 collective-permute-done.6
  273.0 1.9 add.138.total_ref
  276.3 5.4 fusion.x_ref.bc_ref.raw_ref.refs_4_.gate_ref.refs_3_.refs_5_
  281.7 2.2 copy-done.1
  283.9 12.9 %collective-permute-start.7 = (bf16[2,8,1280]{2,1,0:T(8,128)(2,1)S(1)}, bf16[2,8,1280]{2,1,0:T(8,128)(2,1)S(1)}, u32[]{:S(2)}, u32[]{:S(2)}) collective-permute-start(bf16[2,8,1280]{2,1,0:T(8,128)(2,1)S(1)} %slice.503), channel_id=1, source_target_pairs={{0,1},{1,2},{2,3},{4,5},{5,6},{6,7},{8,9},{9,10},{10,11},{12,13},{... | collective-permute-start | bytes 122888 | tf_op jit(solution)/shard_map/ppermute | solution.py:550
  299.7 18.7 %forward_local.3 = (f32[2,256,1024]{2,1,0:T(8,128)}, bf16[2,144,1024]{2,1,0:T(8,128)(2,1)}, f32[2,256,256]{2,1,0:T(8,128)}, f32[2,256,128]{2,1,0:T(8,128)}) custom-call(f32[2,256,2432]{2,1,0:T(8,128)} %copy-done.1, f32[2,256,2432]{2,1,0:T(8,128)} %copy-done.1, f32[2,256,2432]{2,1,0:T(8,128)} %copy-done.1, ...), custom_call_target="tpu_custom_call" | custom-call | flops 4294967296 | bytes 6291456 | tf_op jit(solution)/shard_map/forward_local/pallas_call | solution.py:425
  318.4 5.1 collective-permute-start.8
  323.5 1.3 collective-permute-start.9
  324.8 1.6 collective-permute-start.10
  326.6 21.7 %all-gather.12.cloned.1.call-done.refs_9_.wout_ref = bf16[1024,1024]{1,0:T(8,128)(2,1)} async-done(((bf16[64,1024]{1,0:T(8,128)(2,1)}), bf16[1024,1024]{1,0:T(8,128)(2,1)}) %all-gather.12.cloned.1.call-update) | async-done | bytes 2097168 | tf_op jit(solution)/shard_map/all_gather | solution.py:567
  348.3 8.5 %collective-permute-done.9.refs_1_ = bf16[2,144,1024]{2,1,0:T(8,128)(2,1)S(1)} collective-permute-done((bf16[2,144,1024]{2,1,0:T(8,128)(2,1)}, bf16[2,144,1024]{2,1,0:T(8,128)(2,1)S(1)}, u32[]{:S(2)}, u32[]{:S(2)}) %collective-permute-start.9) | collective-permute-done | bytes 589856 | tf_op jit(solution)/shard_map/ppermute | solution.py:550
  357.7 11.5 %forward_join.3 = (f32[2,256,1024]{2,1,0:T(8,128)}, bf16[2,128,1024]{2,1,0:T(8,128)(2,1)}, f32[2,256,1152]{2,1,0:T(8,128)}) custom-call(bf16[2,144,1024]{2,1,0:T(8,128)(2,1)} %copy-done.19, bf16[2,144,1024]{2,1,0:T(8,128)(2,1)} %copy-done.21, bf16[2,144,1024]{2,1,0:T(8,128)(2,1)} %collective-permute-done.10.refs_2_, ...), custom_call_target="tpu_custom_call" | custom-call | tf_op jit(solution)/shard_map/forward_join/pallas_call | solution.py:452
  369.2 4.7 collective-permute-done.11
  374.0 3.5 add.142.total_ref
  377.5 11.2 %backward_gate.2 = (f32[2,256,1024]{2,1,0:T(8,128)}, bf16[2,256,1024]{2,1,0:T(8,128)(2,1)}, bf16[2,256,1024]{2,1,0:T(8,128)(2,1)}, f32[2,8,1024]{2,1,0:T(8,128)}, bf16[2,144,1024]{2,1,0:T(8,128)(2,1)}) custom-call(bf16[2,256,1024]{2,1,0:T(8,128)(2,1)} %bitcast.133, bf16[1024,1024]{1,0:T(8,128)(2,1)} %all-gather.12.cloned.1.call-done.refs_9_.wout_ref, ...), custom_call_target="tpu_custom_call" | custom-call | tf_op jit(solution)/shard_map/backward_gate/pallas_call | solution.py:474
  388.7 2.5 collective-permute-start.12
  392.4 1.5 collective-permute-start.14
  393.9 3.9 convolution_convert_fusion
  397.9 10.0 %collective-permute-done.12.refs_0_ = bf16[2,144,1024]{2,1,0:T(8,128)(2,1)} collective-permute-done((bf16[2,144,1024]{2,1,0:T(8,128)(2,1)}, bf16[2,144,1024]{2,1,0:T(8,128)(2,1)}, u32[]{:S(2)}, u32[]{:S(2)}) %collective-permute-start.12) | collective-permute-done | bytes 589856 | tf_op jit(solution)/shard_map/ppermute | solution.py:550
  407.9 17.4 %collective-permute-done.13.refs_1_ = bf16[2,144,1024]{2,1,0:T(8,128)(2,1)} collective-permute-done((bf16[2,144,1024]{2,1,0:T(8,128)(2,1)}, bf16[2,144,1024]{2,1,0:T(8,128)(2,1)}, u32[]{:S(2)}, u32[]{:S(2)}) %collective-permute-start.13) | collective-permute-done | bytes 589856 | tf_op jit(solution)/shard_map/ppermute | solution.py:550
  425.3 27.1 %backward_local.2 = (f32[2,256,1024]{2,1,0:T(8,128)}, f32[2,256,256]{2,1,0:T(8,128)}, f32[2,256,128]{2,1,0:T(8,128)}, f32[2,8,1024]{2,1,0:T(8,128)}, f32[2,8,256...) custom-call(bf16[2,144,1024]{2,1,0:T(8,128)(2,1)} %collective-permute-done.12.refs_0_, ...), custom_call_target="tpu_custom_call" | custom-call | tf_op jit(solution)/shard_map/backward_local/pallas_call | solution.py:502
  453.3 22.0 %collective-permute-start.15 = (f32[2,8,1280]{2,1,0:T(8,128)S(1)}, f32[2,8,1280]{2,1,0:T(8,128)S(1)}, u32[]{:S(2)}, u32[]{:S(2)}) collective-permute-start(f32[2,8,1280]{2,1,0:T(8,128)S(1)} %pad_maximum_fusion.1), channel_id=1, source_target_pairs={{1,0},{2,1},{3,2},{5,4},{6,5},{7,6},{9,8},{10,9},{11,10},{13,12},{... | collective-permute-start | bytes 245768 | tf_op jit(solution)/shard_map/ppermute | solution.py:550
  475.3 2.0 collective-permute-done.15.edge_ref
  478.0 7.7 backward_project.2
  485.7 4.4 collective-permute-done.16
  490.1 2.3 fusion.13
  492.4 1.7 fusion.10.grad_ref
  494.1 11.2 %backward_gate.3 = (f32[2,256,1024]{2,1,0:T(8,128)}, bf16[2,256,1024]{2,1,0:T(8,128)(2,1)}, bf16[2,256,1024]{2,1,0:T(8,128)(2,1)}, f32[2,8,1024]{2,1,0:T(8,128)}, bf16[2,144,1024]{2,1,0:T(8,128)(2,1)}) custom-call(bf16[2,256,1024]{2,1,0:T(8,128)(2,1)} %fusion.10.grad_ref, bf16[1024,1024]{1,0:T(8,128)(2,1)} %all-gather.8.cloned.1.call-done.refs_9_.wout_ref, ...), custom_call_target="tpu_custom_call" | custom-call | tf_op jit(solution)/shard_map/backward_gate/pallas_call | solution.py:474
  505.3 3.8 bitcast_convert_fusion.2
  509.4 6.5 bitcast_convert_fusion
  517.0 4.3 collective-permute-start.17
  523.3 25.1 %collective-permute-done.17.refs_0_ = bf16[2,144,1024]{2,1,0:T(8,128)(2,1)S(1)} collective-permute-done((bf16[2,144,1024]{2,1,0:T(8,128)(2,1)S(1)}, bf16[2,144,1024]{2,1,0:T(8,128)(2,1)S(1)}, u32[]{:S(2)}, u32[]{:S(2)}) %collective-permute-start.17) | collective-permute-done | bytes 589856 | tf_op jit(solution)/shard_map/ppermute | solution.py:550
  548.4 11.2 %collective-permute-done.18.refs_1_ = bf16[2,144,1024]{2,1,0:T(8,128)(2,1)S(1)} collective-permute-done((bf16[2,144,1024]{2,1,0:T(8,128)(2,1)S(1)}, bf16[2,144,1024]{2,1,0:T(8,128)(2,1)S(1)}, u32[]{:S(2)}, u32[]{:S(2)}) %collective-permute-start.18) | collective-permute-done | bytes 589856 | tf_op jit(solution)/shard_map/ppermute | solution.py:550
  560.6 27.1 %backward_local.3 = (f32[2,256,1024]{2,1,0:T(8,128)}, f32[2,256,256]{2,1,0:T(8,128)}, f32[2,256,128]{2,1,0:T(8,128)}, f32[2,8,1024]{2,1,0:T(8,128)}, f32[2,8,256...) custom-call(bf16[2,144,1024]{2,1,0:T(8,128)(2,1)} %copy-done.17, ...), custom_call_target="tpu_custom_call" | custom-call | tf_op jit(solution)/shard_map/backward_local/pallas_call | solution.py:502
  588.7 27.0 %collective-permute-start.20 = (f32[2,8,1280]{2,1,0:T(8,128)S(1)}, f32[2,8,1280]{2,1,0:T(8,128)S(1)}, u32[]{:S(2)}, u32[]{:S(2)}) collective-permute-start(f32[2,8,1280]{2,1,0:T(8,128)S(1)} %pad_maximum_fusion.2), channel_id=1, source_target_pairs={{1,0},{2,1},{3,2},{5,4},{6,5},{7,6},{9,8},{10,9},{11,10},{13,12},{... | collective-permute-start | bytes 245768 | tf_op jit(solution)/shard_map/ppermute | solution.py:550
  615.7 4.2 collective-permute-done.20.edge_ref
  620.5 7.9 backward_project.3
  628.8 6.8 bitcast_convert_fusion.1
  636.8 3.2 fusion.23
  640.1 2.5 collective-permute-start.24
  642.8 7.7 collective-permute-done.24
  650.5 1.6 collective-permute-start.25
  652.1 3.0 fusion.26
  655.1 1.3 collective-permute-done.25
  656.6 4.3 collective-permute-done.26
  661.0 3.4 fusion.27
  664.4 1.7 collective-permute-done.27
  674.6 34.3 %reduce-scatter.7.cloned.1.call-done = bf16[64,2432]{1,0:T(8,128)(2,1)} async-done(((bf16[1024,2432]{1,0:T(8,128)(2,1)}), bf16[64,2432]{1,0:T(8,128)(2,1)}) %reduce-scatter.7.cloned.1.call-update) | async-done | bytes 311312 | tf_op jit(solution)/shard_map/reduce_scatter | solution.py:571
  708.9 112.7 %reduce-scatter.5.cloned.1.call-done = bf16[64,2432]{1,0:T(8,128)(2,1)} async-done(((bf16[1024,2432]{1,0:T(8,128)(2,1)}), bf16[64,2432]{1,0:T(8,128)(2,1)}) %reduce-scatter.5.cloned.1.call-update) | async-done | bytes 311312 | tf_op jit(solution)/shard_map/reduce_scatter | solution.py:571
  827.0 1.9 copy.245
  828.9 2.0 reshape.439
  (344 shorter events, 58.4 us)
Async XLA Ops:
  8.0 175.2 %all-reduce.6.cloned.1.call-start = ((), (), s32[]{:S(2)}) async-start(), calls=%async_computation.12 | async-start | bytes 262144
  11.7 7.7 copy-start.42
  11.7 7.8 copy-start.44
  11.7 7.8 copy-start.48
  11.7 7.8 copy-start.49
  11.7 7.9 copy-start.45
  11.7 7.9 copy-start.46
  11.7 7.9 copy-start.47
  19.3 1.9 collective-permute-start
  20.5 166.7 %all-gather.6.cloned.1.call-start = ((), (), s32[]{:S(2)}) async-start(), calls=%async_computation.4 | async-start | bytes 5292032 | tf_op jit(solution)/shard_map/all_gather | solution.py:567
  22.1 207.0 %all-gather.8.cloned.1.call-start = ((), (), s32[]{:S(2)}) async-start(), calls=%async_computation.5 | async-start | bytes 2228224 | tf_op jit(solution)/shard_map/all_gather | solution.py:567
  22.2 1.5 collective-permute-start.5
  24.5 251.8 %all-gather.10.cloned.1.call-start = ((), (), s32[]{:S(2)}) async-start(), calls=%async_computation.6 | async-start | bytes 5292032 | tf_op jit(solution)/shard_map/all_gather | solution.py:567
  25.1 323.2 %all-gather.12.cloned.1.call-start = ((), (), s32[]{:S(2)}) async-start(), calls=%async_computation.7 | async-start | bytes 2228224 | tf_op jit(solution)/shard_map/all_gather | solution.py:567
  187.2 14.4 %copy-start.38 = (f32[2,256]{1,0:T(2,128)S(1)}, f32[2,256]{1,0:T(2,128)}, u32[]{:S(2)}) copy-start(f32[2,256]{1,0:T(2,128)} %get-tuple-element.301) | copy-start | bytes 6148
  194.5 6.5 collective-permute-start.1
  221.5 30.9 %collective-permute-start.2 = (bf16[2,144,1024]{2,1,0:T(8,128)(2,1)}, bf16[2,144,1024]{2,1,0:T(8,128)(2,1)S(1)}, u32[]{:S(2)}, u32[]{:S(2)}) collective-permute-start(bf16[2,144,1024]{2,1,0:T(8,128)(2,1)} %get-tuple-element.103), channel_id=1, source_target_pairs={{0,1},{1,2},{2,3},{4,5},{5,6},{6,7},{8,9},{9,10},{10,11},{12,13},{... | collective-permute-start | bytes 1769480 | tf_op jit(solution)/shard_map/ppermute | solution.py:550
  226.1 29.5 %collective-permute-start.3 = (bf16[2,144,1024]{2,1,0:T(8,128)(2,1)}, bf16[2,144,1024]{2,1,0:T(8,128)(2,1)S(1)}, u32[]{:S(2)}, u32[]{:S(2)}) collective-permute-start(bf16[2,144,1024]{2,1,0:T(8,128)(2,1)} %get-tuple-element.103), channel_id=1, source_target_pairs={{0,2},{1,3},{4,6},{5,7},{8,10},{9,11},{12,14},{13,15},{16,18},{17,... | collective-permute-start | bytes 1769480 | tf_op jit(solution)/shard_map/ppermute | solution.py:550
  227.5 28.2 %collective-permute-start.4 = (bf16[2,144,1024]{2,1,0:T(8,128)(2,1)}, bf16[2,144,1024]{2,1,0:T(8,128)(2,1)S(1)}, u32[]{:S(2)}, u32[]{:S(2)}) collective-permute-start(bf16[2,144,1024]{2,1,0:T(8,128)(2,1)} %get-tuple-element.103), channel_id=1, source_target_pairs={{0,3},{4,7},{8,11},{12,15},{16,19},{20,23},{24,27},{28,31}} | collective-permute-start | bytes 1769480 | tf_op jit(solution)/shard_map/ppermute | solution.py:550
  268.1 4.8 collective-permute-start.6
  268.2 401.0 %reduce-scatter.11.cloned.1.call-start = ((), (), s32[]{:S(2)}) async-start(), calls=%async_computation.11 | async-start | bytes 2228224 | tf_op jit(solution)/shard_map/reduce_scatter | solution.py:571
  276.2 233.2 %copy-start.5 = (bf16[2,256,1024]{2,1,0:T(8,128)(2,1)}, bf16[2,256,1024]{2,1,0:T(8,128)(2,1)S(1)}, u32[]{:S(2)}) copy-start(bf16[2,256,1024]{2,1,0:T(8,128)(2,1)S(1)} %get-tuple-element.269) | copy-start | bytes 3145732
  276.3 20.5 %copy-start.31 = (f32[8,256]{1,0:T(8,128)S(1)}, f32[8,256]{1,0:T(8,128)}, u32[]{:S(2)}) copy-start(f32[8,256]{1,0:T(8,128)} %slice.402) | copy-start | bytes 24580
  276.3 21.1 %copy-start.43 = (f32[96]{0:T(128)S(1)}, f32[96]{0:T(128)}, u32[]{:S(2)}) copy-start(f32[96]{0:T(128)} %get-tuple-element.254) | copy-start | bytes 1156
  283.9 14.5 %collective-permute-start.7 = (bf16[2,8,1280]{2,1,0:T(8,128)(2,1)S(1)}, bf16[2,8,1280]{2,1,0:T(8,128)(2,1)S(1)}, u32[]{:S(2)}, u32[]{:S(2)}) collective-permute-start(bf16[2,8,1280]{2,1,0:T(8,128)(2,1)S(1)} %slice.503), channel_id=1, source_target_pairs={{0,1},{1,2},{2,3},{4,5},{5,6},{6,7},{8,9},{9,10},{10,11},{12,13},{... | collective-permute-start | bytes 122888 | tf_op jit(solution)/shard_map/ppermute | solution.py:550
  299.7 26.8 %copy-start.32 = (f32[16,64]{1,0:T(8,128)S(1)}, f32[16,64]{1,0:T(8,128)}, u32[]{:S(2)}) copy-start(f32[16,64]{1,0:T(8,128)} %get-tuple-element.318) | copy-start | bytes 12292
  318.4 29.9 %collective-permute-start.8 = (bf16[2,144,1024]{2,1,0:T(8,128)(2,1)}, bf16[2,144,1024]{2,1,0:T(8,128)(2,1)S(1)}, u32[]{:S(2)}, u32[]{:S(2)}) collective-permute-start(bf16[2,144,1024]{2,1,0:T(8,128)(2,1)} %get-tuple-element.108), channel_id=1, source_target_pairs={{0,1},{1,2},{2,3},{4,5},{5,6},{6,7},{8,9},{9,10},{10,11},{12,13},{... | collective-permute-start | bytes 1769480 | tf_op jit(solution)/shard_map/ppermute | solution.py:550
  323.5 33.3 %collective-permute-start.9 = (bf16[2,144,1024]{2,1,0:T(8,128)(2,1)}, bf16[2,144,1024]{2,1,0:T(8,128)(2,1)S(1)}, u32[]{:S(2)}, u32[]{:S(2)}) collective-permute-start(bf16[2,144,1024]{2,1,0:T(8,128)(2,1)} %get-tuple-element.108), channel_id=1, source_target_pairs={{0,2},{1,3},{4,6},{5,7},{8,10},{9,11},{12,14},{13,15},{16,18},{17,... | collective-permute-start | bytes 1769480 | tf_op jit(solution)/shard_map/ppermute | solution.py:550
  324.8 32.0 %collective-permute-start.10 = (bf16[2,144,1024]{2,1,0:T(8,128)(2,1)}, bf16[2,144,1024]{2,1,0:T(8,128)(2,1)}, u32[]{:S(2)}, u32[]{:S(2)}) collective-permute-start(bf16[2,144,1024]{2,1,0:T(8,128)(2,1)} %get-tuple-element.108), channel_id=1, source_target_pairs={{0,3},{4,7},{8,11},{12,15},{16,19},{20,23},{24,27},{28,31}} | collective-permute-start | bytes 1769480 | tf_op jit(solution)/shard_map/ppermute | solution.py:550
  348.3 9.2 %copy-start.19 = (bf16[2,144,1024]{2,1,0:T(8,128)(2,1)}, bf16[2,144,1024]{2,1,0:T(8,128)(2,1)S(1)}, u32[]{:S(2)}) copy-start(bf16[2,144,1024]{2,1,0:T(8,128)(2,1)S(1)} %collective-permute-done.8.refs_0_) | copy-start | bytes 1769476
  369.2 4.8 collective-permute-start.11
  377.5 16.4 %copy-start.10 = (bf16[2,1,256,1024]{3,2,1,0:T(8,128)(2,1)S(1)}, bf16[2,1,256,1024]{3,2,1,0:T(8,128)(2,1)}, u32[]{:S(2)}) copy-start(bf16[2,1,256,1024]{3,2,1,0:T(8,128)(2,1)} %param.21) | copy-start | bytes 3145732
  388.7 19.2 %collective-permute-start.12 = (bf16[2,144,1024]{2,1,0:T(8,128)(2,1)}, bf16[2,144,1024]{2,1,0:T(8,128)(2,1)}, u32[]{:S(2)}, u32[]{:S(2)}) collective-permute-start(bf16[2,144,1024]{2,1,0:T(8,128)(2,1)} %get-tuple-element.115), channel_id=1, source_target_pairs={{1,0},{2,1},{3,2},{5,4},{6,5},{7,6},{9,8},{10,9},{11,10},{13,12},{... | collective-permute-start | bytes 1769480 | tf_op jit(solution)/shard_map/ppermute | solution.py:550
  391.1 34.2 %collective-permute-start.13 = (bf16[2,144,1024]{2,1,0:T(8,128)(2,1)}, bf16[2,144,1024]{2,1,0:T(8,128)(2,1)}, u32[]{:S(2)}, u32[]{:S(2)}) collective-permute-start(bf16[2,144,1024]{2,1,0:T(8,128)(2,1)} %get-tuple-element.115), channel_id=1, source_target_pairs={{2,0},{3,1},{6,4},{7,5},{10,8},{11,9},{14,12},{15,13},{18,16},{19,... | collective-permute-start | bytes 1769480 | tf_op jit(solution)/shard_map/ppermute | solution.py:550
  392.4 32.9 %collective-permute-start.14 = (bf16[2,144,1024]{2,1,0:T(8,128)(2,1)}, bf16[2,144,1024]{2,1,0:T(8,128)(2,1)}, u32[]{:S(2)}, u32[]{:S(2)}) collective-permute-start(bf16[2,144,1024]{2,1,0:T(8,128)(2,1)} %get-tuple-element.115), channel_id=1, source_target_pairs={{3,0},{7,4},{11,8},{15,12},{19,16},{23,20},{27,24},{31,28}} | collective-permute-start | bytes 1769480 | tf_op jit(solution)/shard_map/ppermute | solution.py:550
  397.8 271.4 %reduce-scatter.9.cloned.1.call-start = ((), (), s32[]{:S(2)}) async-start(), calls=%async_computation.10 | async-start | bytes 2228224 | tf_op jit(solution)/shard_map/reduce_scatter | solution.py:571
  453.3 24.0 %collective-permute-start.15 = (f32[2,8,1280]{2,1,0:T(8,128)S(1)}, f32[2,8,1280]{2,1,0:T(8,128)S(1)}, u32[]{:S(2)}, u32[]{:S(2)}) collective-permute-start(f32[2,8,1280]{2,1,0:T(8,128)S(1)} %pad_maximum_fusion.1), channel_id=1, source_target_pairs={{1,0},{2,1},{3,2},{5,4},{6,5},{7,6},{9,8},{10,9},{11,10},{13,12},{... | collective-permute-start | bytes 245768 | tf_op jit(solution)/shard_map/ppermute | solution.py:550
  485.7 6.7 copy-start.9
  485.7 4.4 collective-permute-start.16
  494.1 11.2 %copy-start.6 = (bf16[2,256,1024]{2,1,0:T(8,128)(2,1)S(1)}, bf16[2,256,1024]{2,1,0:T(8,128)(2,1)}, u32[]{:S(2)}) copy-start(bf16[2,256,1024]{2,1,0:T(8,128)(2,1)} %fusion.10.grad_ref) | copy-start | bytes 3145732
  509.2 199.8 %reduce-scatter.7.cloned.1.call-start = ((), (), s32[]{:S(2)}) async-start(), calls=%async_computation.9 | async-start | bytes 5292032 | tf_op jit(solution)/shard_map/reduce_scatter | solution.py:571
  516.0 305.7 %reduce-scatter.5.cloned.1.call-start = ((), (), s32[]{:S(2)}) async-start(), calls=%async_computation.8 | async-start | bytes 5292032 | tf_op jit(solution)/shard_map/reduce_scatter | solution.py:571
  517.0 31.4 %collective-permute-start.17 = (bf16[2,144,1024]{2,1,0:T(8,128)(2,1)S(1)}, bf16[2,144,1024]{2,1,0:T(8,128)(2,1)S(1)}, u32[]{:S(2)}, u32[]{:S(2)}) collective-permute-start(bf16[2,144,1024]{2,1,0:T(8,128)(2,1)S(1)} %copy-done.50), channel_id=1, source_target_pairs={{1,0},{2,1},{3,2},{5,4},{6,5},{7,6},{9,8},{10,9},{11,10},{13,12},{... | collective-permute-start | bytes 1769480 | tf_op jit(solution)/shard_map/ppermute | solution.py:550
  521.3 38.3 %collective-permute-start.18 = (bf16[2,144,1024]{2,1,0:T(8,128)(2,1)S(1)}, bf16[2,144,1024]{2,1,0:T(8,128)(2,1)S(1)}, u32[]{:S(2)}, u32[]{:S(2)}) collective-permute-start(bf16[2,144,1024]{2,1,0:T(8,128)(2,1)S(1)} %copy-done.50), channel_id=1, source_target_pairs={{2,0},{3,1},{6,4},{7,5},{10,8},{11,9},{14,12},{15,13},{18,16},{19,... | collective-permute-start | bytes 1769480 | tf_op jit(solution)/shard_map/ppermute | solution.py:550
  522.6 37.0 %collective-permute-start.19 = (bf16[2,144,1024]{2,1,0:T(8,128)(2,1)S(1)}, bf16[2,144,1024]{2,1,0:T(8,128)(2,1)S(1)}, u32[]{:S(2)}, u32[]{:S(2)}) collective-permute-start(bf16[2,144,1024]{2,1,0:T(8,128)(2,1)S(1)} %copy-done.50), channel_id=1, source_target_pairs={{3,0},{7,4},{11,8},{15,12},{19,16},{23,20},{27,24},{31,28}} | collective-permute-start | bytes 1769480 | tf_op jit(solution)/shard_map/ppermute | solution.py:550
  548.4 11.2 %copy-start.17 = (bf16[2,144,1024]{2,1,0:T(8,128)(2,1)}, bf16[2,144,1024]{2,1,0:T(8,128)(2,1)S(1)}, u32[]{:S(2)}) copy-start(bf16[2,144,1024]{2,1,0:T(8,128)(2,1)S(1)} %collective-permute-done.17.refs_0_) | copy-start | bytes 1769476
  588.7 31.2 %collective-permute-start.20 = (f32[2,8,1280]{2,1,0:T(8,128)S(1)}, f32[2,8,1280]{2,1,0:T(8,128)S(1)}, u32[]{:S(2)}, u32[]{:S(2)}) collective-permute-start(f32[2,8,1280]{2,1,0:T(8,128)S(1)} %pad_maximum_fusion.2), channel_id=1, source_target_pairs={{1,0},{2,1},{3,2},{5,4},{6,5},{7,6},{9,8},{10,9},{11,10},{13,12},{... | collective-permute-start | bytes 245768 | tf_op jit(solution)/shard_map/ppermute | solution.py:550
  620.5 7.9 copy-start.26
  620.5 8.0 copy-start.27
  620.5 8.0 copy-start.35
  620.5 8.0 copy-start.40
  628.4 8.3 collective-permute-start.21
  628.4 7.1 copy-start.30
  640.1 10.3 %collective-permute-start.24 = (f32[2,8496]{1,0:T(2,128)S(1)}, f32[2,8496]{1,0:T(2,128)S(1)}, u32[]{:S(2)}, u32[]{:S(2)}) collective-permute-start(f32[2,8496]{1,0:T(2,128)S(1)} %pad_maximum_fusion.4), channel_id=1, source_target_pairs={{0,1},{1,0},{2,3},{3,2},{4,5},{5,4},{6,7},{7,6},{8,9},{9,8},{10,11... | collective-permute-start | bytes 203912 | tf_op jit(solution)/shard_map/ppermute | solution.py:561
  650.5 10.5 %copy-start.7 = (bf16[2,256,1024]{2,1,0:T(8,128)(2,1)S(1)}, bf16[2,256,1024]{2,1,0:T(8,128)(2,1)}, u32[]{:S(2)}) copy-start(bf16[2,256,1024]{2,1,0:T(8,128)(2,1)} %fusion.10.grad_ref) | copy-start | bytes 3145732
  650.5 10.5 %copy-start.8 = (f32[2,256,1024]{2,1,0:T(8,128)S(1)}, f32[2,256,1024]{2,1,0:T(8,128)}, u32[]{:S(2)}) copy-start(f32[2,256,1024]{2,1,0:T(8,128)} %get-tuple-element.134) | copy-start | bytes 6291460
  650.5 10.5 %copy-start.37 = (f32[2,256]{1,0:T(2,128)S(1)}, f32[2,256]{1,0:T(2,128)}, u32[]{:S(2)}) copy-start(f32[2,256]{1,0:T(2,128)} %get-tuple-element.308) | copy-start | bytes 6148
  650.5 5.9 collective-permute-start.25
  656.5 4.4 collective-permute-start.26
  660.9 5.3 collective-permute-start.27
  666.4 1.3 collective-permute-start.28
  670.2 3.5 collective-permute-start.23
  708.9 115.5 %copy-start.12 = (bf16[64,2432]{1,0:T(8,128)(2,1)S(1)}, bf16[64,2432]{1,0:T(8,128)(2,1)}, u32[]{:S(2)}) copy-start(bf16[64,2432]{1,0:T(8,128)(2,1)} %reduce-scatter.7.cloned.1.call-done) | copy-start | bytes 933892
  822.7 1.7 collective-permute-start.22
  (26 other events, 49.0 us)
Sparse Core Ops, SparseCore 0:
  20.6 162.5 all-reduce.5
Sparse Core Ops, SparseCore 1:
  24.3 83.8 all-gather.5
  110.8 59.3 all-gather.7
  172.7 97.1 all-gather.9
  272.6 75.6 all-gather.11
  397.9 75.8 reduce-scatter.10
  509.3 75.5 reduce-scatter.8
  587.0 121.9 reduce-scatter.6
  711.2 110.4 reduce-scatter.4
